TPU v7x, 512 devices: a whole 4x4x16 slice. The times are simulated.
512 devices in a mesh: seq: 32 (over y, z_lo), ch: 16 (over x, z_hi, core).
Axes of the slice: x: 4, y: 4, z: 16 (z_hi: 2, z_lo: 8; z = z_hi * 8 + z_lo), core: 2. Of those that a mesh axis runs over, the one named last changes fastest.
Arguments:
- query_act: bfloat16 [8192, 8192], P('seq', 'ch'), may hold values from -6 to 6
- key_act: bfloat16 [8192, 8192], P('seq', 'ch'), may hold values from -6 to 6
- value_act: bfloat16 [8192, 8192], P('seq', 'ch'), may hold values from -110 to 110
- conv_out: bfloat16 [8192, 8192], P('seq', 'ch'), may hold values from -110 to 110
- grad_out: bfloat16 [8192, 8192], P('seq', 'ch'), may hold values from -6 to 6
- norm_gain: float32 [16, 512], P('ch'), may hold values from 0.5 to 1.5
- skip_gain: float32 [16, 512], P('ch', 'seq'), may hold values from 0.25 to 2
- filters: float32 [16, 512, 8192], P('ch', 'seq'), may hold values from -6 to 6
- row_prev: float32 [16, 8192], P('ch', 'seq'), may hold values from 0.1 to 2
- col_prev: float32 [16, 512], P('ch', 'seq'), may hold values from 0.1 to 2
Outputs:
- grad_query: bfloat16 [8192, 8192], P('seq', 'ch')
- grad_key: bfloat16 [8192, 8192], P('seq', 'ch')
- grad_value: bfloat16 [8192, 8192], P('seq', 'ch')
- grad_filters: float32 [16, 512, 8192], P('ch', 'seq')
- grad_gain: float32 [16, 512], P('ch', 'seq')
- grad_skip: float32 [16, 512], P('ch', 'seq')
- row_moment: float32 [16, 8192], P('ch', 'seq')
- col_moment: float32 [16, 512], P('ch', 'seq')
All inputs are finite; a program needn't handle non-finite values.
Results may differ from a plain program's by a relative error of at most 0.013.
Values may be sent and summed in bfloat16 or wider, within the bound.
No kernel may reach another device: no remote copies, remote signals or barrier semaphores. Data moves between devices by JAX's collectives and lax.ppermute only.
A program may use at most 64 MiB of HBM per device.

v0:
```python
import math

import jax
import jax.numpy as jnp
from jax import lax
from jax.sharding import PartitionSpec as P

EPS_NORM = 1e-05
EPS_MOMENT = 1e-30
DECAY = 1.0 - 2.0 ** (-0.8)
HIGHEST = lax.Precision.HIGHEST


def dft_tables(seq_span):
    inner_len = min(128, seq_span)
    half_len = seq_span // inner_len
    outer_len = 2 * half_len
    padded_len = outer_len * inner_len
    outer_idx = jnp.arange(outer_len, dtype=jnp.int32)
    half_idx = jnp.arange(half_len, dtype=jnp.int32)
    inner_idx = jnp.arange(inner_len, dtype=jnp.int32)
    first_phase = (outer_idx[:, None] * half_idx[None, :] % outer_len).astype(jnp.float32) * (
        -2.0 * math.pi / outer_len
    )
    twist_phase = (outer_idx[:, None] * inner_idx[None, :] % padded_len).astype(jnp.float32) * (
        -2.0 * math.pi / padded_len
    )
    inner_phase = (inner_idx[:, None] * inner_idx[None, :] % inner_len).astype(jnp.float32) * (
        -2.0 * math.pi / inner_len
    )
    return (
        jnp.cos(first_phase),
        jnp.sin(first_phase),
        jnp.cos(twist_phase),
        jnp.sin(twist_phase),
        jnp.cos(inner_phase),
        jnp.sin(inner_phase),
    )


def right_mult(left, table):
    return jnp.einsum("ckm,mj->ckj", left, table, precision=HIGHEST)


def forward_dft(signal, tables):
    cos_outer, sin_outer, twist_re, twist_im, inner_re, inner_im = tables
    shaped = signal.reshape(cos_outer.shape[1], inner_re.shape[0], signal.shape[1])
    section_re = jnp.einsum("kn,nmc->ckm", cos_outer, shaped, precision=HIGHEST)
    section_im = jnp.einsum("kn,nmc->ckm", sin_outer, shaped, precision=HIGHEST)
    turned_re = section_re * twist_re - section_im * twist_im
    turned_im = section_re * twist_im + section_im * twist_re
    spec_re = right_mult(turned_re, inner_re) - right_mult(turned_im, inner_im)
    spec_im = right_mult(turned_re, inner_im) + right_mult(turned_im, inner_re)
    return (spec_re, spec_im)


def inverse_dft(spec_re, spec_im, tables):
    cos_outer, sin_outer, twist_re, twist_im, inner_re, inner_im = tables
    back_re = right_mult(spec_re, inner_re) + right_mult(spec_im, inner_im)
    back_im = right_mult(spec_im, inner_re) - right_mult(spec_re, inner_im)
    turned_re = back_re * twist_re + back_im * twist_im
    turned_im = back_im * twist_re - back_re * twist_im
    signal = jnp.einsum("kn,ckm->nmc", cos_outer, turned_re, precision=HIGHEST)
    signal = signal + jnp.einsum("kn,ckm->nmc", sin_outer, turned_im, precision=HIGHEST)
    padded_len = cos_outer.shape[0] * inner_re.shape[0]
    return (signal / padded_len).reshape(-1, signal.shape[2])


def correlate(first, second, tables):
    prod_re = first[0] * second[0] + first[1] * second[1]
    prod_im = first[1] * second[0] - first[0] * second[1]
    return inverse_dft(prod_re, prod_im, tables)


def spectral(conv_cols, mixed_cols, filt_rows, skip_row, filt_scale):
    tables = dft_tables(conv_cols.shape[0])
    conv32 = conv_cols.astype(jnp.float32)
    mixed32 = mixed_cols.astype(jnp.float32)
    conv_spec = forward_dft(conv32, tables)
    filt_spec = forward_dft(filt_rows.T * filt_scale, tables)
    mixed_spec = forward_dft(mixed32, tables)
    grad_mix = correlate(conv_spec, filt_spec, tables) + skip_row[None, :] * conv32
    grad_filt = correlate(conv_spec, mixed_spec, tables) * filt_scale
    grad_skip = jnp.sum(conv32 * mixed32, axis=0)
    return (grad_mix, grad_filt, grad_skip)


def body(
    query_act,
    key_act,
    value_act,
    conv_out,
    grad_out,
    norm_gain,
    skip_gain,
    filters,
    row_prev,
    col_prev,
):
    tok_rows = query_act.shape[0]
    seq_span = filters.shape[2]
    group_width = query_act.shape[1]
    total_width = group_width * lax.axis_size("ch")
    filt_scale = 1.0 / math.sqrt(seq_span)
    query32 = query_act.astype(jnp.float32)
    conv32 = conv_out.astype(jnp.float32)
    gated_out = query32 * conv32
    cotangent = grad_out.astype(jnp.float32)
    scaled = cotangent * norm_gain
    square_part = jnp.sum(gated_out * gated_out, axis=1)
    dot_part = jnp.sum(scaled * gated_out, axis=1)
    square_sum, dot_sum = lax.psum((square_part, dot_part), "ch")
    inv_rms = lax.rsqrt(square_sum / total_width + EPS_NORM)[:, None]
    mean_dot = (dot_sum / total_width)[:, None]
    gain_part = jnp.sum(cotangent * gated_out * inv_rms, axis=0)
    grad_gain = lax.psum_scatter(gain_part, "seq", scatter_dimension=0, tiled=True).reshape(1, -1)
    grad_gated = inv_rms * (scaled - gated_out * inv_rms * inv_rms * mean_dot)
    grad_query = (grad_gated * conv32).astype(jnp.bfloat16)
    grad_conv = (grad_gated * query32).astype(jnp.bfloat16)
    filt_rows = filters[0]
    skip_row = skip_gain[0]
    keys_cols, values_cols, conv_cols = (
        lax.all_to_all(key_act, "seq", split_axis=1, concat_axis=0, tiled=True),
        lax.all_to_all(value_act, "seq", split_axis=1, concat_axis=0, tiled=True),
        lax.all_to_all(grad_conv, "seq", split_axis=1, concat_axis=0, tiled=True),
    )
    keys_wide = keys_cols.astype(jnp.float32)
    values_wide = values_cols.astype(jnp.float32)
    mixed_cols = (keys_wide * values_wide).astype(jnp.bfloat16)
    grad_mix, grad_filt, grad_skip = spectral(
        conv_cols, mixed_cols, filt_rows, skip_row, filt_scale
    )
    key_cols = (grad_mix * values_wide).astype(jnp.bfloat16)
    value_cols = (grad_mix * keys_wide).astype(jnp.bfloat16)
    grad_key, grad_value = (
        lax.all_to_all(key_cols, "seq", split_axis=0, concat_axis=1, tiled=True),
        lax.all_to_all(value_cols, "seq", split_axis=0, concat_axis=1, tiled=True),
    )
    squares = grad_filt * grad_filt + EPS_MOMENT
    row_part = jnp.sum(squares, axis=1)
    row_total = lax.psum(row_part.astype(jnp.bfloat16), "seq").astype(jnp.float32)
    row_mine = lax.dynamic_slice_in_dim(row_total, lax.axis_index("seq") * tok_rows, tok_rows)
    row_moment = DECAY * row_prev + (1.0 - DECAY) * (row_mine / group_width)[None, :]
    col_moment = DECAY * col_prev + (1.0 - DECAY) * jnp.mean(squares, axis=0)[None, :]
    grad_filters = grad_filt.T[None]
    return (
        grad_query,
        grad_key,
        grad_value,
        grad_filters,
        grad_gain,
        grad_skip[None],
        row_moment,
        col_moment,
    )


def solution(mesh):
    placed = (
        P("seq", "ch"),
        P("seq", "ch"),
        P("seq", "ch"),
        P("seq", "ch"),
        P("seq", "ch"),
        P("ch", None),
        P("ch", "seq"),
        P("ch", "seq", None),
        P("ch", "seq"),
        P("ch", "seq"),
    )
    return jax.shard_map(
        body,
        mesh=mesh,
        in_specs=placed,
        out_specs=(
            P("seq", "ch"),
            P("seq", "ch"),
            P("seq", "ch"),
            P("ch", "seq", None),
            P("ch", "seq"),
            P("ch", "seq"),
            P("ch", "seq"),
            P("ch", "seq"),
        ),
        check_vma=False,
    )
```

profile of v0, /device:TPU:0, one launch (start us, length us, event | category | flops | bytes accessed | tf_op | source)
XLA Modules:
  0.0 635.1 jit_solution(12710934325332194139)
XLA Ops:
  0.6 1.8 copy.144
  2.4 10.3 %all-to-all-start.3 = ((bf16[256,32,16]{0,2,1:T(8,128)(2,1)}), bf16[256,32,16]{0,2,1:T(8,128)(2,1)S(1)}, u32[]{:S(2)}, u32[]{:S(2)}) async-start(bf16[256,32,16]{0,2,1:T(8,128)(2,1)} %bitcast.19), calls=%async_computation.3 | async-start | bytes 524288 | tf_op jit(solution)/shard_map/all_to_all | solution.py:123
  14.9 69.6 %psum.21 = f32[256]{0:T(256)S(1)} all-reduce(f32[256]{0:T(256)S(1)} %multiply_reduce_fusion), channel_id=1, replica_groups=mesh['seq'=32,'ch'=16] {'ch'}, use_global_device_ids=true, to_apply=%region_1.0 | all-reduce | flops 256 | bytes 2048 | tf_op jit(solution)/shard_map/psum | solution.py:112
  85.5 62.1 %psum.22 = f32[256]{0:T(256)S(1)} all-reduce(f32[256]{0:T(256)S(1)} %get-tuple-element.33), channel_id=1, replica_groups=mesh['seq'=32,'ch'=16] {'ch'}, use_global_device_ids=true, to_apply=%region_3.0 | all-reduce | flops 256 | bytes 2048 | tf_op jit(solution)/shard_map/psum | solution.py:112
  151.3 1.3 dynamic-slice
  153.2 123.4 %all-reduce = f32[512]{0:T(512)S(1)} all-reduce(f32[512]{0:T(512)S(1)} %get-tuple-element.32), channel_id=2, replica_groups=mesh['seq'=32,'ch'=16] {'seq'}, use_global_device_ids=true, to_apply=%region_5.0.clone | all-reduce | flops 512 | bytes 4096
  276.6 1.8 convolution_bitcast_fusion
  278.4 1.8 convolution_bitcast_fusion.1
  280.3 4.8 all-to-all-start.1
  285.6 2.0 fusion.46
  287.7 3.0 fusion.47
  290.7 2.0 convolution_add_fusion.3
  292.7 8.1 %all-to-all-done.1 = bf16[256,32,16]{0,2,1:T(8,128)(2,1)} async-done(((bf16[256,32,16]{0,2,1:T(8,128)(2,1)}), bf16[256,32,16]{0,2,1:T(8,128)(2,1)}, u32[]{:S(2)}, u32[]{:S(2)}) %all-to-all-start.1) | async-done | bytes 262176 | tf_op jit(solution)/shard_map/all_to_all | solution.py:124
  300.8 7.0 %all-to-all-start = ((bf16[256,32,16]{0,2,1:T(8,128)(2,1)}), bf16[256,32,16]{0,2,1:T(8,128)(2,1)}, u32[]{:S(2)}, u32[]{:S(2)}) async-start(bf16[256,32,16]{0,2,1:T(8,128)(2,1)} %bitcast.178), calls=%async_computation | async-start | bytes 524288 | tf_op jit(solution)/shard_map/all_to_all | solution.py:125
  307.8 4.2 convolution_subtract_fusion.3
  312.1 1.0 fusion.50
  314.7 1.7 convolution_bitcast_fusion.3
  316.4 6.9 %all-to-all-done = bf16[256,32,16]{0,2,1:T(8,128)(2,1)} async-done(((bf16[256,32,16]{0,2,1:T(8,128)(2,1)}), bf16[256,32,16]{0,2,1:T(8,128)(2,1)}, u32[]{:S(2)}, u32[]{:S(2)}) %all-to-all-start) | async-done | bytes 262176 | tf_op jit(solution)/shard_map/all_to_all | solution.py:125
  323.3 1.7 copy.125
  325.0 1.7 reshape.119
  326.8 1.8 convolution_bitcast_fusion.4
  329.3 2.0 fusion.48
  331.3 2.0 fusion.49
  333.3 2.0 fusion.45
  335.3 2.4 fusion.44
  337.8 2.0 convolution_add_fusion.1
  339.8 2.0 convolution_subtract_fusion.4
  341.9 2.0 convolution_subtract_fusion.1
  343.9 2.4 multiply_add_fusion
  346.4 1.3 fusion.71
  347.7 1.5 fusion.73
  349.2 1.3 convolution_subtract_fusion.2
  350.6 1.3 convolution_add_fusion.2
  351.9 1.5 fusion.13
  353.4 1.5 fusion.2
  355.7 2.8 fusion.31
  358.6 5.6 all-to-all-start.2
  364.1 1.3 fusion.65
  365.4 1.3 fusion.67
  366.8 1.3 convolution_subtract_fusion
  368.1 1.3 convolution_add_fusion
  369.5 14.6 %all-to-all-done.2 = bf16[32,256,16]{1,2,0:T(8,128)(2,1)S(1)} async-done(((bf16[32,256,16]{1,2,0:T(8,128)(2,1)}), bf16[32,256,16]{1,2,0:T(8,128)(2,1)S(1)}, u32[]{:S(2)}, u32[]{:S(2)}) %all-to-all-start.2) | async-done | bytes 262176 | tf_op jit(solution)/shard_map/all_to_all | solution.py:136
  384.1 5.7 all-to-all-start.4
  389.8 1.5 fusion.6
  391.3 2.1 fusion.42
  393.4 1.1 copy.191
  394.5 235.2 %psum.23 = bf16[8192]{0:T(1024)(128)(2,1)S(1)} all-reduce(bf16[8192]{0:T(1024)(128)(2,1)S(1)} %bitcast.181), channel_id=1, replica_groups=mesh['seq'=32,'ch'=16] {'seq'}, use_global_device_ids=true, to_apply=%region_8.9 | all-reduce | flops 8192 | bytes 32768 | tf_op jit(solution)/shard_map/psum | solution.py:141
  633.0 1.8 copy.158
  (54 shorter events, 13.8 us)
Async XLA Ops:
  2.4 10.3 %copy-start.4 = (bf16[256,512]{1,0:T(8,128)(2,1)S(1)}, bf16[256,512]{1,0:T(8,128)(2,1)}, u32[]{:S(2)}) copy-start(bf16[256,512]{1,0:T(8,128)(2,1)} %param.10) | copy-start | bytes 786436
  2.4 277.8 %all-to-all-start.3 = ((bf16[256,32,16]{0,2,1:T(8,128)(2,1)}), bf16[256,32,16]{0,2,1:T(8,128)(2,1)S(1)}, u32[]{:S(2)}, u32[]{:S(2)}) async-start(bf16[256,32,16]{0,2,1:T(8,128)(2,1)} %bitcast.19), calls=%async_computation.3 | async-start | bytes 524288 | tf_op jit(solution)/shard_map/all_to_all | solution.py:123
  12.7 1.0 copy-start.5
  13.7 0.9 copy-start.6
  84.6 0.7 copy-start.8
  148.6 0.9 copy-start.7
  149.6 1.6 copy-start.3
  280.3 20.5 %all-to-all-start.1 = ((bf16[256,32,16]{0,2,1:T(8,128)(2,1)}), bf16[256,32,16]{0,2,1:T(8,128)(2,1)}, u32[]{:S(2)}, u32[]{:S(2)}) async-start(bf16[256,32,16]{0,2,1:T(8,128)(2,1)} %bitcast.15), calls=%async_computation.1 | async-start | bytes 524288 | tf_op jit(solution)/shard_map/all_to_all | solution.py:124
  300.8 22.5 %all-to-all-start = ((bf16[256,32,16]{0,2,1:T(8,128)(2,1)}), bf16[256,32,16]{0,2,1:T(8,128)(2,1)}, u32[]{:S(2)}, u32[]{:S(2)}) async-start(bf16[256,32,16]{0,2,1:T(8,128)(2,1)} %bitcast.178), calls=%async_computation | async-start | bytes 524288 | tf_op jit(solution)/shard_map/all_to_all | solution.py:125
  313.3 0.7 copy-start.1
  326.8 1.8 copy-start.2
  341.9 2.0 copy-start
  355.1 0.7 copy-start.10
  358.6 25.5 %all-to-all-start.2 = ((bf16[32,256,16]{1,2,0:T(8,128)(2,1)}), bf16[32,256,16]{1,2,0:T(8,128)(2,1)S(1)}, u32[]{:S(2)}, u32[]{:S(2)}) async-start(bf16[32,256,16]{1,2,0:T(8,128)(2,1)} %get-tuple-element.45), calls=%async_computation.2 | async-start | bytes 524288 | tf_op jit(solution)/shard_map/all_to_all | solution.py:136
  384.1 249.0 %all-to-all-start.4 = ((bf16[32,256,16]{1,2,0:T(8,128)(2,1)}), bf16[32,256,16]{1,2,0:T(8,128)(2,1)}, u32[]{:S(2)}, u32[]{:S(2)}) async-start(bf16[32,256,16]{1,2,0:T(8,128)(2,1)} %get-tuple-element.44), calls=%async_computation.4 | async-start | bytes 524288 | tf_op jit(solution)/shard_map/all_to_all | solution.py:137
  629.8 0.7 copy-start.11
  629.8 0.7 copy-start.12
  631.0 0.7 copy-start.9
where the time goes:
time: 641 us; the launch traced here: 635 us
  blocking collectives  490 us (76%)
  matrix products  54.2 us (8%)
  starting transfers between devices  33.4 us (5%)
  waiting for transfers between devices  29.6 us (5%)
  local copies, waits for them, and re-layouts  18.6 us (3%)
  other arithmetic  6.97 us (1%)
    psum x1, blocking collectives, body(): lax.psum(row_part.astype(jnp.bfloat16), 'seq').astype(jnp.float32)  235 us
    psum x2, blocking collectives, body(): square_sum, dot_sum = lax.psum((square_part, dot_part), 'ch')  132 us
    unnamed x1, blocking collectives  123 us
    dot_general x20, matrix products, right_mult(): return jnp.einsum('ckm,mj->ckj', left, table, precision=HIGHEST)  39.1 us
    all_to_all x1, waiting for transfers between devices, body(): lax.all_to_all(key_cols, 'seq', split_axis=0, concat_axis=1, tiled=True)  14.6 us
    unnamed x37, local copies, waits for them, and re-layouts  14.1 us
  transfers between devices with their start and end apart: 5, of which 3 were waited for; matrix products, arithmetic and copies ran while one was open for 6% of the time, Pallas kernels for 0%

commit v1 on v0

v1 whole, which is shorter than its diff:
```python
import functools
import math

import jax
import jax.numpy as jnp
from jax import lax
from jax.experimental import pallas as pl
from jax.experimental.pallas import tpu as pltpu
from jax.sharding import PartitionSpec as P

EPS_NORM = 1e-05
EPS_MOMENT = 1e-30
DECAY = 1.0 - 2.0 ** (-0.8)
F32 = jnp.float32
BF16 = jnp.bfloat16
LANE = 128
VMEM_LIMIT = 48 << 20


def iota(shape, axis):
    return lax.broadcasted_iota(jnp.int32, shape, axis)


def reversal():
    return jnp.where(iota((LANE, LANE), 0) + iota((LANE, LANE), 1) == LANE - 1, 1.0, 0.0).astype(BF16)


def kernel_call(body, outs, args, scratch=(), flops=0):
    total = sum(math.prod(a.shape) * a.dtype.itemsize for a in list(args) + list(outs))
    return pl.pallas_call(
        body,
        out_shape=tuple(outs),
        in_specs=[pl.BlockSpec(memory_space=pltpu.VMEM)] * len(args),
        out_specs=tuple(pl.BlockSpec(memory_space=pltpu.VMEM) for _ in outs),
        scratch_shapes=list(scratch),
        compiler_params=pltpu.CompilerParams(vmem_limit_bytes=VMEM_LIMIT),
        cost_estimate=pl.CostEstimate(flops=flops, bytes_accessed=total, transcendentals=0),
    )(*args)


def shape(dims, dtype):
    return jax.ShapeDtypeStruct(dims, dtype)


def token_sums(query, conv, cot, gain, out):
    gated = query[...].astype(F32) * conv[...].astype(F32)
    scaled = cot[...].astype(F32) * gain[...]
    width = gated.shape[1]

    def fold(x):
        part = sum(x[:, k : k + LANE] for k in range(0, width, LANE))
        cols = [
            jnp.sum(part[r : r + LANE].T, axis=0, keepdims=True) for r in range(0, part.shape[0], LANE)
        ]
        return jnp.concatenate(cols, axis=1)

    both = jnp.concatenate([fold(gated * gated), fold(scaled * gated)], axis=0)
    for peer in range(out.shape[0]):
        out[peer] = both


def mix_columns(key, value, out):
    mixed = (key[...].astype(F32) * value[...].astype(F32)).astype(BF16).astype(F32)
    flip = reversal()
    for cb in range(mixed.shape[1] // LANE):
        for half in range(mixed.shape[0] // LANE):
            block = mixed[half * LANE : (half + 1) * LANE, cb * LANE : (cb + 1) * LANE].T.astype(BF16)
            block = jnp.dot(block, flip, preferred_element_type=F32).astype(BF16)
            for d in range(8):
                out[cb * 8 + d, half * 16 : half * 16 + 16, :] = block[d * 16 : d * 16 + 16, :]


def filter_rows(filt, out):
    flip = reversal()
    for b in range(filt.shape[1] // LANE):
        block = filt[:, b * LANE : (b + 1) * LANE].astype(BF16)
        out[b * 16 : b * 16 + 16, :] = jnp.dot(block, flip, preferred_element_type=F32).astype(BF16)


def token_grads(total_width, query, conv, cot, gain, sums, grad_query, conv_cols, gain_part):
    totals = jnp.sum(sums[...], axis=0)
    inv_row = lax.rsqrt(totals[0:1, :] / total_width + EPS_NORM)
    back_row = inv_row * inv_row * (totals[1:2, :] / total_width)
    rows = query.shape[0]
    both = jnp.concatenate([inv_row, back_row, jnp.zeros((6, rows), F32)], axis=0)
    for half in range(rows // LANE):
        lo = half * LANE
        cols = jnp.concatenate([both[:, lo : lo + LANE]] * (LANE // 8), axis=0).T
        inv = cols[:, 0:1]
        back = cols[:, 1:2]
        for cb in range(query.shape[1] // LANE):
            at = (slice(lo, lo + LANE), slice(cb * LANE, (cb + 1) * LANE))
            query32 = query[at].astype(F32)
            conv32 = conv[at].astype(F32)
            cot32 = cot[at].astype(F32)
            gated = query32 * conv32
            grad = inv * (cot32 * gain[:, at[1]] - gated * back)
            grad_query[at] = (grad * conv32).astype(BF16)
            block = (grad * query32).T.astype(BF16)
            for d in range(8):
                conv_cols[cb * 8 + d, half * 16 : half * 16 + 16, :] = block[d * 16 : d * 16 + 16, :]
            part = jnp.sum(cot32 * gated * inv, axis=0, keepdims=True)
            if half == 0:
                gain_part[:, at[1]] = part
            else:
                gain_part[:, at[1]] += part


def correlations(
    n_blocks, scale, group, conv_cols, mixed_cols, filt, skip, gain_part, col_prev,
    back, grad_filt, grad_skip, col_moment,
    conv_s, mix_s, filt_s, hankel, conv_c, cols_c, mix_out, filt_out,
):
    chans = 16
    peers = n_blocks // 2
    row, lane = iota((LANE, LANE), 0), iota((LANE, LANE), 1)
    keep = lane <= row
    for d in range(peers):
        at = slice(d * 32, d * 32 + 32)
        conv_s[at, :] = conv_cols[d].astype(F32)
        mix_s[at, :] = mixed_cols[d].astype(F32)
        filt_s[at, :] = filt[at, :].astype(F32)
    for b in range(2):
        conv_c[b, n_blocks : n_blocks + 8, :] = jnp.zeros((8, LANE), F32)
        for i in range(2):
            cols_c[b, i, 0:n_blocks, :] = jnp.zeros((n_blocks, LANE), F32)

    def build(c, b):
        conv_c[b, 0:n_blocks, :] = conv_s[pl.ds(c, n_blocks, stride=chans), :]
        cols_c[b, 0, n_blocks:, :] = filt_s[pl.ds(c, n_blocks, stride=chans), :]
        cols_c[b, 1, n_blocks:, :] = mix_s[pl.ds(c, n_blocks, stride=chans), :]

        def turned(k):
            wide = jnp.broadcast_to(conv_c[b, k : k + 1, :], (LANE, LANE))
            return pltpu.roll(wide, 1, axis=1, stride=1, stride_axis=0)

        now = turned(0)
        for k in range(n_blocks):
            later = turned(k + 1)
            hankel[b, k * LANE : (k + 1) * LANE, :] = jnp.where(keep, now, later).astype(BF16)
            now = later

    def dots(c, b):
        total = None
        cuts = 4
        step = n_blocks // 2 // cuts
        for q in reversed(range(cuts)):
            rows = n_blocks // cuts * (q + 1)
            skipped = n_blocks - rows
            part = None
            for p in range(step * q, step * (q + 1)):
                halves = []
                for half in range(2):
                    at = 2 * p + half + 1 + skipped
                    halves.append(
                        jnp.concatenate([cols_c[b, i, at : at + rows, :] for i in range(2)], axis=0).astype(BF16)
                    )
                got = jnp.dot(
                    jnp.concatenate(halves, axis=1),
                    hankel[b, 2 * LANE * p : 2 * LANE * (p + 1), :],
                    preferred_element_type=F32,
                )
                part = got if part is None else part + got
            if total is None:
                total = part
            else:
                blank = jnp.zeros((skipped, LANE), F32)
                total = total + jnp.concatenate([blank, part[:rows], blank, part[rows:]], axis=0)
        mix_out[pl.ds(c, n_blocks, stride=chans), :] = total[:n_blocks]
        filt_out[pl.ds(c, n_blocks, stride=chans), :] = total[n_blocks:]

    build(0, 0)

    def pair(i, carry):
        c = 2 * i
        build(c + 1, 1)
        dots(c, 0)
        build(jnp.minimum(c + 2, chans - 1), 0)
        dots(c + 1, 1)
        return carry

    lax.fori_loop(0, chans // 2, pair, 0)

    diagonal = iota((chans, LANE), 0) == iota((chans, LANE), 1)

    def to_lanes(x):
        return jnp.sum(jnp.where(diagonal, jnp.sum(x, axis=1, keepdims=True), 0.0), axis=0, keepdims=True)

    skip_col = jnp.sum(jnp.where(diagonal, jnp.concatenate([skip[...], jnp.zeros((1, LANE - chans), F32)], axis=1), 0.0), axis=1, keepdims=True)
    skip_sum = jnp.zeros((chans, LANE), F32)
    col_sum = jnp.zeros((chans, LANE), F32)
    flip = reversal()
    for b in range(n_blocks):
        d, half = divmod(b, 2)
        at = slice(b * chans, (b + 1) * chans)
        turned_at = slice((n_blocks - 1 - b) * chans, (n_blocks - b) * chans)
        conv = conv_s[at, :]
        mixed = jnp.dot(mix_s[at, :].astype(BF16), flip, preferred_element_type=F32)
        skip_sum = skip_sum + conv * mixed
        back[d, half * 16 : half * 16 + 16, :] = (mix_out[turned_at, :] * scale + skip_col * conv).astype(BF16)
        grad = filt_out[turned_at, :] * scale
        grad_filt[:, b * LANE : (b + 1) * LANE] = grad
        squares = grad * grad + EPS_MOMENT
        col_sum = col_sum + squares
        lag_part = jnp.sum(squares, axis=0, keepdims=True)
        if half == 0:
            first = lag_part
            continue
        tile = gain_part[:, d // 8 * LANE : (d // 8 + 1) * LANE]
        high = tile.astype(BF16).astype(F32)
        low = (tile - high).astype(BF16).astype(F32)
        rest = tile - high - low
        extra = jnp.concatenate([first, lag_part, high, low, rest, jnp.zeros((3, LANE), F32)], axis=0)
        back[d, 32:40, :] = extra.astype(BF16)
    grad_skip[...] = to_lanes(skip_sum)[:, :chans]
    mean = to_lanes(col_sum)[:, :chans] / (n_blocks * LANE)
    col_moment[...] = DECAY * col_prev[...] + (1.0 - DECAY) * mean


def finish(group, back, key, value, row_prev, grad_key, grad_value, row_moment, gain_tile):
    for half in range(key.shape[0] // LANE):
        for cb in range(key.shape[1] // LANE):
            at = (slice(half * LANE, (half + 1) * LANE), slice(cb * LANE, (cb + 1) * LANE))
            block = jnp.concatenate(
                [back[cb * 8 + d, half * 16 : half * 16 + 16, :].astype(F32) for d in range(8)], axis=0
            ).T
            grad_key[at] = (block * value[at].astype(F32)).astype(BF16)
            grad_value[at] = (block * key[at].astype(F32)).astype(BF16)
    extra = jnp.zeros((8, LANE), F32)
    for d in range(back.shape[0]):
        extra = extra + back[d, 32:40, :].astype(F32)
    lags = jnp.concatenate([extra[0:1], extra[1:2]], axis=1)
    row_moment[...] = DECAY * row_prev[...] + (1.0 - DECAY) * (lags / group)
    gain_tile[...] = extra[2:3] + extra[3:4] + extra[4:5]


def body(query, key, value, conv, cot, norm_gain, skip_gain, filters, row_prev, col_prev):
    rows, group = query.shape
    n_seq, n_ch = lax.axis_size("seq"), lax.axis_size("ch")
    chans, span = filters.shape[1:]
    n_blocks = span // LANE
    filt = filters[0]
    (sums,) = kernel_call(
        token_sums, [shape((n_ch, 2, rows), F32)], [query, conv, cot, norm_gain]
    )
    (mix_cols,) = kernel_call(mix_columns, [shape((n_seq, 32, LANE), BF16)], [key, value])
    (filt_rows,) = kernel_call(filter_rows, [shape((n_blocks * chans, LANE), BF16)], [filt])
    sums = lax.all_to_all(sums, "ch", split_axis=0, concat_axis=0, tiled=True)
    mix_cols = lax.all_to_all(mix_cols, "seq", split_axis=0, concat_axis=0, tiled=True)
    grad_query, conv_cols, gain_part = kernel_call(
        functools.partial(token_grads, group * n_ch),
        [shape((rows, group), BF16), shape((n_seq, 32, LANE), BF16), shape((1, group), F32)],
        [query, conv, cot, norm_gain, sums],
    )
    conv_cols = lax.all_to_all(conv_cols, "seq", split_axis=0, concat_axis=0, tiled=True)
    back, grad_filt, grad_skip, col_moment = kernel_call(
        functools.partial(correlations, n_blocks, 1.0 / math.sqrt(span), group),
        [
            shape((n_seq, 40, LANE), BF16),
            shape((chans, span), F32),
            shape((1, chans), F32),
            shape((1, chans), F32),
        ],
        [conv_cols, mix_cols, filt_rows, skip_gain, gain_part, col_prev],
        [
            pltpu.VMEM((n_blocks * chans, LANE), F32),
            pltpu.VMEM((n_blocks * chans, LANE), F32),
            pltpu.VMEM((n_blocks * chans, LANE), F32),
            pltpu.VMEM((2, span, LANE), BF16),
            pltpu.VMEM((2, n_blocks + 8, LANE), F32),
            pltpu.VMEM((2, 2, 2 * n_blocks, LANE), F32),
            pltpu.VMEM((n_blocks * chans, LANE), F32),
            pltpu.VMEM((n_blocks * chans, LANE), F32),
        ],
        flops=2 * chans * span * span,
    )
    back = lax.all_to_all(back, "seq", split_axis=0, concat_axis=0, tiled=True)
    grad_key, grad_value, row_moment, gain_tile = kernel_call(
        functools.partial(finish, group),
        [
            shape((rows, group), BF16),
            shape((rows, group), BF16),
            shape((1, rows), F32),
            shape((1, LANE), F32),
        ],
        [back, key, value, row_prev],
    )
    mine = lax.rem(lax.axis_index("seq"), 8) * chans
    grad_gain = lax.dynamic_slice_in_dim(gain_tile, mine, chans, axis=1)
    return grad_query, grad_key, grad_value, grad_filt[None], grad_gain, grad_skip, row_moment, col_moment


def solution(mesh):
    tokens = P("seq", "ch")
    owned = P("ch", "seq")
    spread = P("ch", "seq", None)
    return jax.shard_map(
        body,
        mesh=mesh,
        in_specs=(tokens,) * 5 + (P("ch", None), owned, spread, owned, owned),
        out_specs=(tokens,) * 3 + (spread, owned, owned, owned, owned),
        check_vma=False,
    )
```

time: 641 us -> 133 us (0.21)
  the two profiles are of different devices: /device:TPU:0 before, /device:TPU:1 now
where the time goes in v1:
time: 133 us
  waiting for transfers between devices  70.4 us (53%)
  starting transfers between devices  37.4 us (28%)
  Pallas kernels  20.1 us (15%)
  local copies, waits for them, and re-layouts  4.15 us (3%)
    all_to_all x1, waiting for transfers between devices, body(): back = lax.all_to_all(back, 'seq', split_axis=0, concat_axis=0, tiled=True)  21.4 us
    pallas_call x6, Pallas kernels, kernel_call(): pl.pallas_call(body, out_shape=tuple(outs), in_specs=[pl.BlockSpec(memory...  20.1 us
    all_to_all x1, starting transfers between devices, body(): sums = lax.all_to_all(sums, 'ch', split_axis=0, concat_axis=0, tiled=True)  19.1 us
    all_to_all x1, waiting for transfers between devices, body(): lax.all_to_all(conv_cols, 'seq', split_axis=0, concat_axis=0, tiled=True)  18.1 us
    all_to_all x1, waiting for transfers between devices, body(): lax.all_to_all(mix_cols, 'seq', split_axis=0, concat_axis=0, tiled=True)  17.5 us
    all_to_all x1, waiting for transfers between devices, body(): sums = lax.all_to_all(sums, 'ch', split_axis=0, concat_axis=0, tiled=True)  13.5 us
    all_to_all x1, starting transfers between devices, body(): lax.all_to_all(mix_cols, 'seq', split_axis=0, concat_axis=0, tiled=True)  7.77 us
    all_to_all x1, starting transfers between devices, body(): lax.all_to_all(conv_cols, 'seq', split_axis=0, concat_axis=0, tiled=True)  5.32 us
  transfers between devices with their start and end apart: 4, of which 4 were waited for; matrix products, arithmetic and copies ran while one was open for 0% of the time, Pallas kernels for 2%

profile of v1, /device:TPU:1, one launch (start us, length us, event | category | flops | bytes accessed | tf_op | source)
XLA Modules:
  0.0 132.8 jit_solution(3743952810817085318)
XLA Ops:
  0.6 0.0 copy-start
  0.6 0.9 copy-done
  1.6 0.0 copy-start.2
  1.6 0.9 copy-done.2
  2.5 0.0 copy-start.4
  2.5 0.9 copy-done.4
  3.5 0.0 copy-start.9
  3.5 0.7 copy-done.9
  4.2 0.0 copy-start.6
  4.2 0.0 copy-start.7
  4.2 0.8 shard_map.161
  5.0 19.1 %all-to-all-start = ((f32[16,2,256]{2,1,0:T(2,128)}), f32[16,2,256]{2,1,0:T(2,128)S(1)}, u32[]{:S(2)}, u32[]{:S(2)}) async-start(f32[16,2,256]{2,1,0:T(2,128)} %shard_map.161), calls=%async_computation | async-start | bytes 65536 | tf_op jit(solution)/shard_map/all_to_all | solution.py:248
  24.1 0.0 copy-done.6
  24.1 0.0 copy-done.7
  24.1 0.0 copy-start.5
  24.1 0.0 copy-start.10
  24.1 1.0 shard_map.163
  25.1 0.0 copy-start.1
  25.1 0.0 copy-start.3
  25.1 13.5 %all-to-all-done.sums = f32[16,2,256]{2,1,0:T(2,128)S(1)} async-done(((f32[16,2,256]{2,1,0:T(2,128)}), f32[16,2,256]{2,1,0:T(2,128)S(1)}, u32[]{:S(2)}, u32[]{:S(2)}) %all-to-all-start) | async-done | bytes 32800 | tf_op jit(solution)/shard_map/all_to_all | solution.py:248
  38.6 7.8 %all-to-all-start.2 = ((bf16[32,32,128]{2,1,0:T(8,128)(2,1)}), bf16[32,32,128]{2,1,0:T(8,128)(2,1)S(1)}, u32[]{:S(2)}, u32[]{:S(2)}) async-start(bf16[32,32,128]{2,1,0:T(8,128)(2,1)} %shard_map.163), calls=%async_computation.2 | async-start | bytes 524288 | tf_op jit(solution)/shard_map/all_to_all | solution.py:249
  46.4 0.0 copy-done.5
  46.4 0.0 copy-done.10
  46.4 0.0 copy-done.1
  46.4 0.0 copy-done.3
  46.4 0.0 copy-start.8
  46.4 1.2 shard_map.162
  47.7 17.5 %all-to-all-done.2.mixed_cols = bf16[32,32,128]{2,1,0:T(8,128)(2,1)S(1)} async-done(((bf16[32,32,128]{2,1,0:T(8,128)(2,1)}), bf16[32,32,128]{2,1,0:T(8,128)(2,1)S(1)}, u32[]{:S(2)}, u32[]{:S(2)}) %all-to-all-start.2) | async-done | bytes 262176 | tf_op jit(solution)/shard_map/all_to_all | solution.py:249
  65.2 5.3 %all-to-all-start.1 = ((bf16[32,32,128]{2,1,0:T(8,128)(2,1)}), bf16[32,32,128]{2,1,0:T(8,128)(2,1)S(1)}, u32[]{:S(2)}, u32[]{:S(2)}) async-start(bf16[32,32,128]{2,1,0:T(8,128)(2,1)} %get-tuple-element.20), calls=%async_computation.1 | async-start | bytes 524288 | tf_op jit(solution)/shard_map/all_to_all | solution.py:255
  70.5 0.0 copy-done.8
  70.5 0.6 shard_map.164.filt
  71.1 0.0 copy-start.12
  71.1 0.0 copy-start.13
  71.1 18.1 %all-to-all-done.1.conv_cols = bf16[32,32,128]{2,1,0:T(8,128)(2,1)S(1)} async-done(((bf16[32,32,128]{2,1,0:T(8,128)(2,1)}), bf16[32,32,128]{2,1,0:T(8,128)(2,1)S(1)}, u32[]{:S(2)}, u32[]{:S(2)}) %all-to-all-start.1) | async-done | bytes 262176 | tf_op jit(solution)/shard_map/all_to_all | solution.py:255
  89.2 0.0 copy-done.12
  89.2 0.0 copy-done.13
  89.2 15.4 %shard_map.165 = (bf16[32,40,128]{2,1,0:T(8,128)(2,1)}, f32[16,8192]{1,0:T(8,128)}, f32[1,16]{1,0:T(1,128)}, f32[1,16]{1,0:T(1,128)}) custom-call(bf16[32,32,128]{2,1,0:T(8,128)(2,1)S(1)} %all-to-all-done.1.conv_cols, bf16[32,32,128]{2,1,0:T(8,128)(2,1)S(1)} %all-to-all-done.2.mixed_cols, bf16[1024,128]{1,0:T(8,128)(2,1)S(1)} %shard_map.164.filt, ...), custom_call_target="tpu_custom_call" | custom-call | flops 2147483648 | bytes 1640704 | tf_op jit(solution)/shard_map/pallas_call | solution.py:30
  104.6 5.2 %all-to-all-start.3 = ((bf16[32,40,128]{2,1,0:T(8,128)(2,1)}), bf16[32,40,128]{2,1,0:T(8,128)(2,1)S(1)}, u32[]{:S(2)}, u32[]{:S(2)}) async-start(bf16[32,40,128]{2,1,0:T(8,128)(2,1)} %get-tuple-element.22), calls=%async_computation.3 | async-start | bytes 655360 | tf_op jit(solution)/shard_map/all_to_all | solution.py:277
  109.9 0.0 copy-start.11
  109.9 21.4 %all-to-all-done.3.back = bf16[32,40,128]{2,1,0:T(8,128)(2,1)S(1)} async-done(((bf16[32,40,128]{2,1,0:T(8,128)(2,1)}), bf16[32,40,128]{2,1,0:T(8,128)(2,1)S(1)}, u32[]{:S(2)}, u32[]{:S(2)}) %all-to-all-start.3) | async-done | bytes 327712 | tf_op jit(solution)/shard_map/all_to_all | solution.py:277
  131.3 0.0 copy-done.11
  131.3 1.0 shard_map.166
  132.3 0.6 constant_dynamic-slice_fusion
Async XLA Ops:
  0.6 1.0 copy-start
  1.6 0.9 copy-start.2
  2.5 0.9 copy-start.4
  3.5 0.7 copy-start.9
  4.2 19.9 %copy-start.6 = (bf16[256,512]{1,0:T(8,128)(2,1)S(1)}, bf16[256,512]{1,0:T(8,128)(2,1)}, u32[]{:S(2)}) copy-start(bf16[256,512]{1,0:T(8,128)(2,1)} %key.3) | copy-start | bytes 786436
  4.2 19.9 %copy-start.7 = (bf16[256,512]{1,0:T(8,128)(2,1)S(1)}, bf16[256,512]{1,0:T(8,128)(2,1)}, u32[]{:S(2)}) copy-start(bf16[256,512]{1,0:T(8,128)(2,1)} %value.3) | copy-start | bytes 786436
  5.0 33.6 %all-to-all-start = ((f32[16,2,256]{2,1,0:T(2,128)}), f32[16,2,256]{2,1,0:T(2,128)S(1)}, u32[]{:S(2)}, u32[]{:S(2)}) async-start(f32[16,2,256]{2,1,0:T(2,128)} %shard_map.161), calls=%async_computation | async-start | bytes 65536 | tf_op jit(solution)/shard_map/all_to_all | solution.py:248
  24.1 22.3 %copy-start.5 = (bf16[256,512]{1,0:T(8,128)(2,1)S(1)}, bf16[256,512]{1,0:T(8,128)(2,1)}, u32[]{:S(2)}) copy-start(bf16[256,512]{1,0:T(8,128)(2,1)} %cot.3) | copy-start | bytes 786436
  24.1 22.3 %copy-start.10 = (f32[1,512]{1,0:T(1,128)S(1)}, f32[1,512]{1,0:T(1,128)}, u32[]{:S(2)}) copy-start(f32[1,512]{1,0:T(1,128)} %gain.3) | copy-start | bytes 6148
  25.1 21.3 %copy-start.1 = (bf16[256,512]{1,0:T(8,128)(2,1)S(1)}, bf16[256,512]{1,0:T(8,128)(2,1)}, u32[]{:S(2)}) copy-start(bf16[256,512]{1,0:T(8,128)(2,1)} %query.3) | copy-start | bytes 786436
  25.1 21.3 %copy-start.3 = (bf16[256,512]{1,0:T(8,128)(2,1)S(1)}, bf16[256,512]{1,0:T(8,128)(2,1)}, u32[]{:S(2)}) copy-start(bf16[256,512]{1,0:T(8,128)(2,1)} %conv.3) | copy-start | bytes 786436
  38.6 26.6 %all-to-all-start.2 = ((bf16[32,32,128]{2,1,0:T(8,128)(2,1)}), bf16[32,32,128]{2,1,0:T(8,128)(2,1)S(1)}, u32[]{:S(2)}, u32[]{:S(2)}) async-start(bf16[32,32,128]{2,1,0:T(8,128)(2,1)} %shard_map.163), calls=%async_computation.2 | async-start | bytes 524288 | tf_op jit(solution)/shard_map/all_to_all | solution.py:249
  46.4 24.1 %copy-start.8 = (f32[1,16,8192]{2,1,0:T(8,128)S(1)}, f32[1,16,8192]{2,1,0:T(8,128)}, u32[]{:S(2)}) copy-start(f32[1,16,8192]{2,1,0:T(8,128)} %param.17) | copy-start | bytes 1572868
  65.2 24.1 %all-to-all-start.1 = ((bf16[32,32,128]{2,1,0:T(8,128)(2,1)}), bf16[32,32,128]{2,1,0:T(8,128)(2,1)S(1)}, u32[]{:S(2)}, u32[]{:S(2)}) async-start(bf16[32,32,128]{2,1,0:T(8,128)(2,1)} %get-tuple-element.20), calls=%async_computation.1 | async-start | bytes 524288 | tf_op jit(solution)/shard_map/all_to_all | solution.py:255
  71.1 18.1 %copy-start.12 = (f32[1,16]{1,0:T(1,128)S(1)}, f32[1,16]{1,0:T(1,128)}, u32[]{:S(2)}) copy-start(f32[1,16]{1,0:T(1,128)} %skip.1) | copy-start | bytes 196
  71.1 18.1 %copy-start.13 = (f32[1,16]{1,0:T(1,128)S(1)}, f32[1,16]{1,0:T(1,128)}, u32[]{:S(2)}) copy-start(f32[1,16]{1,0:T(1,128)} %col_prev.1) | copy-start | bytes 196
  104.6 26.6 %all-to-all-start.3 = ((bf16[32,40,128]{2,1,0:T(8,128)(2,1)}), bf16[32,40,128]{2,1,0:T(8,128)(2,1)S(1)}, u32[]{:S(2)}, u32[]{:S(2)}) async-start(bf16[32,40,128]{2,1,0:T(8,128)(2,1)} %get-tuple-element.22), calls=%async_computation.3 | async-start | bytes 655360 | tf_op jit(solution)/shard_map/all_to_all | solution.py:277
  109.9 21.4 %copy-start.11 = (f32[1,256]{1,0:T(1,128)S(1)}, f32[1,256]{1,0:T(1,128)}, u32[]{:S(2)}) copy-start(f32[1,256]{1,0:T(1,128)} %row_prev.1) | copy-start | bytes 3076

commit v2 on v1

v2 whole, which is shorter than its diff:
```python
import functools
import math

import jax
import jax.numpy as jnp
from jax import lax
from jax.experimental import pallas as pl
from jax.experimental.pallas import tpu as pltpu
from jax.sharding import PartitionSpec as P

EPS_NORM = 1e-05
EPS_MOMENT = 1e-30
DECAY = 1.0 - 2.0 ** (-0.8)
F32 = jnp.float32
BF16 = jnp.bfloat16
LANE = 128


def iota(shape, axis):
    return lax.broadcasted_iota(jnp.int32, shape, axis)


STEP = 4
HALF = 64


def residue_order():
    token, lane = iota((2 * LANE, 2 * LANE), 0), iota((2 * LANE, 2 * LANE), 1)
    source = STEP * (HALF - 1 - lane % HALF) + lane // HALF
    return jnp.where(token == source, 1.0, 0.0).astype(BF16)


def kernel_call(body, outs, args, scratch=(), flops=0, in_place=(), vmem=16 << 20):
    total = sum(math.prod(a.shape) * a.dtype.itemsize for a in list(args) + list(outs))
    return pl.pallas_call(
        body,
        out_shape=tuple(outs),
        in_specs=[pl.BlockSpec(memory_space=pl.ANY if i in in_place else pltpu.VMEM) for i in range(len(args))],
        out_specs=tuple(pl.BlockSpec(memory_space=pltpu.VMEM) for _ in outs),
        scratch_shapes=list(scratch),
        compiler_params=pltpu.CompilerParams(vmem_limit_bytes=vmem),
        cost_estimate=pl.CostEstimate(flops=flops, bytes_accessed=total, transcendentals=0),
    )(*args)


def shape(dims, dtype):
    return jax.ShapeDtypeStruct(dims, dtype)


def token_sums(query_at, conv_at, cot_at, gain, out, query, conv, cot, sems):
    copies = [
        pltpu.make_async_copy(src, dst, sems.at[i])
        for i, (src, dst) in enumerate([(query_at, query), (conv_at, conv), (cot_at, cot)])
    ]
    for copy in copies:
        copy.start()
    for copy in copies:
        copy.wait()
    gated = query[...].astype(F32) * conv[...].astype(F32)
    scaled = cot[...].astype(F32) * gain[...]
    width = gated.shape[1]

    def fold(x):
        part = sum(x[:, k : k + LANE] for k in range(0, width, LANE))
        cols = [
            jnp.sum(part[r : r + LANE].T, axis=0, keepdims=True) for r in range(0, part.shape[0], LANE)
        ]
        return jnp.concatenate(cols, axis=1)

    both = jnp.concatenate([fold(gated * gated), fold(scaled * gated)], axis=0)
    for peer in range(out.shape[0]):
        out[peer] = both


def mix_columns(key, value, out):
    mixed = (key[...].astype(F32) * value[...].astype(F32)).astype(BF16).astype(F32)
    order = residue_order()
    for cb in range(mixed.shape[1] // LANE):
        block = mixed[:, cb * LANE : (cb + 1) * LANE].T.astype(BF16)
        block = jnp.dot(block, order, preferred_element_type=F32).astype(BF16)
        for d in range(8):
            for tile in range(2):
                out[cb * 8 + d, tile * 16 : tile * 16 + 16, :] = block[
                    d * 16 : d * 16 + 16, tile * LANE : (tile + 1) * LANE
                ]


def filter_rows(filt, out):
    order = residue_order()
    for n in range(filt.shape[1] // (2 * LANE)):
        block = filt[:, n * 2 * LANE : (n + 1) * 2 * LANE].astype(BF16)
        block = jnp.dot(block, order, preferred_element_type=F32).astype(BF16)
        for tile in range(2):
            out[n, tile * 16 : tile * 16 + 16, :] = block[:, tile * LANE : (tile + 1) * LANE]


def token_grads(total_width, query, conv, cot, gain, near, far, mix_cols, grad_query, cols, gain_part):
    totals = near[...] + far[...]
    inv_row = lax.rsqrt(totals[0:1, :] / total_width + EPS_NORM)
    back_row = inv_row * inv_row * (totals[1:2, :] / total_width)
    rows = query.shape[0]
    cols[:, 32:64, :] = mix_cols[...]
    both = jnp.concatenate([inv_row, back_row, jnp.zeros((6, rows), F32)], axis=0)
    for half in range(rows // LANE):
        lo = half * LANE
        turned = jnp.concatenate([both[:, lo : lo + LANE]] * (LANE // 8), axis=0).T
        inv = turned[:, 0:1]
        back = turned[:, 1:2]
        for cb in range(query.shape[1] // LANE):
            at = (slice(lo, lo + LANE), slice(cb * LANE, (cb + 1) * LANE))
            query32 = query[at].astype(F32)
            conv32 = conv[at].astype(F32)
            cot32 = cot[at].astype(F32)
            gated = query32 * conv32
            grad = inv * (cot32 * gain[:, at[1]] - gated * back)
            grad_query[at] = (grad * conv32).astype(BF16)
            block = (grad * query32).T.astype(BF16)
            for d in range(8):
                cols[cb * 8 + d, half * 16 : half * 16 + 16, :] = block[d * 16 : d * 16 + 16, :]
            part = jnp.sum(cot32 * gated * inv, axis=0, keepdims=True)
            if half == 0:
                gain_part[:, at[1]] = part
            else:
                gain_part[:, at[1]] += part


def correlations(
    scale, cols, filt, skip, gain_part, col_prev,
    back, grad_filt, grad_skip, col_moment,
    conv_s, wide_s, hankel, conv_c, wide_c, mix_out, filt_out,
):
    chans = 16
    peers = cols.shape[0]
    n_tiles = 2 * peers
    segments = 2 * STEP
    lead = 8
    lane = iota((chans, LANE), 1)
    rows_kept = iota((32, LANE), 1) < STEP + STEP * iota((32, LANE), 0)

    def residues(ref, n, first):
        if n < 0 or n >= peers:
            return [jnp.zeros((chans, LANE), F32)] * 2
        return [ref[n, first + tile * 16 : first + tile * 16 + 16, :].astype(F32) for tile in range(2)]

    for d in range(peers):
        conv_s[d * 32 : d * 32 + 32, :] = cols[d, 0:32, :].astype(F32)
    for which, (ref, first) in enumerate([(filt, 0), (cols, 32)]):
        for r in range(STEP):
            wide_s[which * STEP + r, 0 : lead * chans, :] = jnp.zeros((lead * chans, LANE), F32)
        now = residues(ref, -1, first)
        now_rolled = now
        for n in range(-1, peers - 1):
            later = residues(ref, n + 1, first)
            later_rolled = [pltpu.roll(x, HALF, axis=1) for x in later]
            at = slice((lead + n) * chans, (lead + n + 1) * chans)
            for tile in range(2):
                low = which * STEP + 2 * tile
                wide_s[low, at, :] = jnp.where(lane < HALF, now[tile], later_rolled[tile])
                wide_s[low + 1, at, :] = jnp.where(lane < HALF, now_rolled[tile], later[tile])
            now, now_rolled = later, later_rolled
    for b in range(2):
        hankel[b, n_tiles * 32 : (n_tiles + 1) * 32, :] = jnp.zeros((32, LANE), BF16)
        for seg in range(segments):
            wide_c[b, seg, 0 : peers - lead, :] = jnp.zeros((peers - lead, LANE), F32)

    def build(c, b):
        conv_c[b] = conv_s[pl.ds(c, n_tiles, stride=chans), :]
        for seg in range(segments):
            wide_c[b, seg, peers - lead : 2 * peers, :] = wide_s[seg, pl.ds(c, peers + lead, stride=chans), :]

        def turned(k):
            if k == n_tiles:
                return jnp.zeros((32, LANE), F32)
            wide = jnp.broadcast_to(conv_c[b, k : k + 1, :], (32, LANE))
            return pltpu.roll(wide, STEP, axis=1, stride=STEP, stride_axis=0)

        now = turned(0)
        for k in range(n_tiles):
            later = turned(k + 1)
            hankel[b, k * 32 : (k + 1) * 32, :] = jnp.where(rows_kept, now, later).astype(BF16)
            now = later

    def dots(c, b):
        cuts = 4
        total = None
        for q in reversed(range(cuts)):
            rows = peers // cuts * (q + 1)
            skipped = peers - rows
            part = None
            for n in range(peers // cuts * q, peers // cuts * (q + 1), 4):
                left = []
                for half in range(2):
                    at = n + 2 * half + 1 + skipped
                    left.append(
                        jnp.concatenate([wide_c[b, seg, at : at + rows, :] for seg in range(segments)], axis=0).astype(BF16)
                    )
                right = []
                for k in range(2 * n, 2 * n + 8, 2):
                    for t in (k + 1, k):
                        right.append(
                            jnp.concatenate([hankel[b, 32 * t : 32 * t + 32, :], hankel[b, 32 * t + 32 : 32 * t + 64, :]], axis=1)
                        )
                got = jnp.dot(
                    jnp.concatenate(left, axis=1), jnp.concatenate(right, axis=0), preferred_element_type=F32
                )
                part = got if part is None else part + got
            pieces = [part[seg * rows : (seg + 1) * rows] for seg in range(segments)]
            if total is None:
                total = pieces
            else:
                blank = jnp.zeros((skipped, 2 * LANE), F32)
                total = [x + jnp.concatenate([blank, y], axis=0) for x, y in zip(total, pieces)]

        inner = iota((peers, LANE), 1) < LANE - 1
        top = jnp.zeros((1, LANE), F32)

        def later_by_one(x):
            first, second = [pltpu.roll(x[:, t * LANE : (t + 1) * LANE], LANE - 1, axis=1) for t in range(2)]
            below = jnp.concatenate([top, first[:-1]], axis=0)
            return jnp.concatenate([jnp.where(inner, first, second), jnp.where(inner, second, below)], axis=1)

        for which, out in enumerate([mix_out, filt_out]):
            sums = total[which * STEP + STEP - 1]
            for r in reversed(range(STEP - 1)):
                sums = total[which * STEP + r] + later_by_one(sums)
            for tile in range(2):
                out[tile, pl.ds(c, peers, stride=chans), :] = sums[:, tile * LANE : (tile + 1) * LANE]

    build(0, 0)

    def pair(i, carry):
        c = 2 * i
        build(c + 1, 1)
        dots(c, 0)
        build(jnp.minimum(c + 2, chans - 1), 0)
        dots(c + 1, 1)
        return carry

    lax.fori_loop(0, chans // 2, pair, 0)

    diagonal = iota((chans, LANE), 0) == iota((chans, LANE), 1)

    def to_lanes(x):
        return jnp.sum(jnp.where(diagonal, x, 0.0), axis=0, keepdims=True)

    skip_col = jnp.sum(
        jnp.where(diagonal, jnp.concatenate([skip[...], jnp.zeros((1, LANE - chans), F32)], axis=1), 0.0),
        axis=1,
        keepdims=True,
    )
    col_sum = jnp.zeros((chans, LANE), F32)
    for d in range(peers):
        at = slice((peers - 1 - d) * chans, (peers - d) * chans)
        lags = []
        for tile in range(2):
            k = 2 * d + tile
            conv = conv_s[k * chans : (k + 1) * chans, :]
            back[d, tile * 16 : tile * 16 + 16, :] = (mix_out[tile, at, :] * scale + skip_col * conv).astype(BF16)
            grad = filt_out[tile, at, :] * scale
            grad_filt[:, k * LANE : (k + 1) * LANE] = grad
            squares = grad * grad + EPS_MOMENT
            col_sum = col_sum + squares
            lags.append(jnp.sum(squares, axis=0, keepdims=True))
        part = gain_part[:, d // 8 * LANE : (d // 8 + 1) * LANE]
        high = part.astype(BF16).astype(F32)
        low = (part - high).astype(BF16).astype(F32)
        extra = jnp.concatenate(lags + [high, low, part - high - low, jnp.zeros((3, LANE), F32)], axis=0)
        back[d, 32:40, :] = extra.astype(BF16)
    grad_skip[...] = to_lanes(filt_out[0, (peers - 1) * chans : peers * chans, 0:1])[:, :chans]
    mean = to_lanes(jnp.sum(col_sum, axis=1, keepdims=True))[:, :chans] / (n_tiles * LANE)
    col_moment[...] = DECAY * col_prev[...] + (1.0 - DECAY) * mean


def finish(group, back, key, value, row_prev, grad_key, grad_value, row_moment, grad_gain):
    for half in range(key.shape[0] // LANE):
        for cb in range(key.shape[1] // LANE):
            at = (slice(half * LANE, (half + 1) * LANE), slice(cb * LANE, (cb + 1) * LANE))
            block = jnp.concatenate(
                [back[cb * 8 + d, half * 16 : half * 16 + 16, :].astype(F32) for d in range(8)], axis=0
            ).T
            grad_key[at] = (block * value[at].astype(F32)).astype(BF16)
            grad_value[at] = (block * key[at].astype(F32)).astype(BF16)
    extra = jnp.zeros((8, LANE), F32)
    for d in range(back.shape[0]):
        extra = extra + back[d, 32:40, :].astype(F32)
    lags = jnp.concatenate([extra[0:1], extra[1:2]], axis=1)
    row_moment[...] = DECAY * row_prev[...] + (1.0 - DECAY) * (lags / group)
    gains = jnp.broadcast_to(extra[2:3] + extra[3:4] + extra[4:5], (8, LANE))
    chans = grad_gain.shape[1]
    place = lax.rem(lax.axis_index("seq"), LANE // chans)
    grad_gain[...] = pltpu.roll(gains, lax.rem(LANE - place * chans, LANE), axis=1)[0:1, :chans]


def sum_over_channels(sums):
    groups = [[4 * x + 2 * z + core for x in range(4) for core in range(2)] for z in range(2)]
    parts = lax.all_to_all(sums, "ch", split_axis=0, concat_axis=0, axis_index_groups=groups, tiled=True)
    here = jnp.sum(parts, axis=0)
    return here, lax.ppermute(here, "ch", [(i, i ^ 2) for i in range(16)])


def correlate_call(chans, span, peers, args):
    return kernel_call(
        functools.partial(correlations, 1.0 / math.sqrt(span)),
        [
            shape((peers, 40, LANE), BF16),
            shape((chans, span), F32),
            shape((1, chans), F32),
            shape((1, chans), F32),
        ],
        args,
        [
            pltpu.VMEM((2 * peers * chans, LANE), F32),
            pltpu.VMEM((2 * STEP, (peers + 8) * chans, LANE), F32),
            pltpu.VMEM((2, (2 * peers + 1) * 32, LANE), BF16),
            pltpu.VMEM((2, 2 * peers, LANE), F32),
            pltpu.VMEM((2, 2 * STEP, 2 * peers, LANE), F32),
            pltpu.VMEM((2, peers * chans, LANE), F32),
            pltpu.VMEM((2, peers * chans, LANE), F32),
        ],
        flops=2 * chans * span * span,
        vmem=40 << 20,
    )


def body(query, key, value, conv, cot, norm_gain, skip_gain, filters, row_prev, col_prev):
    rows, group = query.shape
    n_seq, n_ch = lax.axis_size("seq"), lax.axis_size("ch")
    chans, span = filters.shape[1:]
    (sums,) = kernel_call(
        token_sums,
        [shape((n_ch // 2, 2, rows), F32)],
        [query, conv, cot, norm_gain],
        [pltpu.VMEM((rows, group), BF16)] * 3 + [pltpu.SemaphoreType.DMA((3,))],
        in_place=(0, 1, 2),
        vmem=60 << 20,
    )
    (mix_cols,) = kernel_call(mix_columns, [shape((n_seq, 32, LANE), BF16)], [key, value])
    (filt_rows,) = kernel_call(filter_rows, [shape((n_seq, 32, LANE), BF16)], [filters[0]])
    near, far = sum_over_channels(sums)
    grad_query, cols, gain_part = kernel_call(
        functools.partial(token_grads, group * n_ch),
        [shape((rows, group), BF16), shape((n_seq, 64, LANE), BF16), shape((1, group), F32)],
        [query, conv, cot, norm_gain, near, far, mix_cols],
    )
    cols = lax.all_to_all(cols, "seq", split_axis=0, concat_axis=0, tiled=True)
    back, grad_filt, grad_skip, col_moment = correlate_call(
        chans, span, n_seq, [cols, filt_rows, skip_gain, gain_part, col_prev]
    )
    back = lax.all_to_all(back, "seq", split_axis=0, concat_axis=0, tiled=True)
    grad_key, grad_value, row_moment, grad_gain = kernel_call(
        functools.partial(finish, group),
        [
            shape((rows, group), BF16),
            shape((rows, group), BF16),
            shape((1, rows), F32),
            shape((1, chans), F32),
        ],
        [back, key, value, row_prev],
    )
    return grad_query, grad_key, grad_value, grad_filt[None], grad_gain, grad_skip, row_moment, col_moment


def solution(mesh):
    tokens = P("seq", "ch")
    owned = P("ch", "seq")
    spread = P("ch", "seq", None)
    return jax.shard_map(
        body,
        mesh=mesh,
        in_specs=(tokens,) * 5 + (P("ch", None), owned, spread, owned, owned),
        out_specs=(tokens,) * 3 + (spread, owned, owned, owned, owned),
        check_vma=False,
    )
```

time: 133 us -> 110 us (0.83)
  blocking collectives: 0 us -> 41.7 us
  waiting for transfers between devices: 70.4 us -> 30.1 us
  starting transfers between devices: 37.4 us -> 22.3 us
  Pallas kernels: 20.1 us -> 14.7 us
  local copies, waits for them, and re-layouts: 4.15 us -> 0.04 us
    all_to_all x4 -> x1, waiting for transfers between devices: 70.4 us -> 28.5 us  [body(): cols = lax.all_to_all(cols, 'seq', split_axis=0, concat_axis=0, tiled=True)]
    all_to_all x0 -> x2, blocking collectives: none -> 41.7 us  [the longest x1 26.9 us: body(): back = lax.all_to_all(back, 'seq', split_axis=0, concat_axis=0, tiled=True)]
    all_to_all x4 -> x1, starting transfers between devices: 37.4 us -> 11.1 us  [body(): cols = lax.all_to_all(cols, 'seq', split_axis=0, concat_axis=0, tiled=True)]
    ppermute x0 -> x1, starting transfers between devices: none -> 11.3 us  [sum_over_channels(): return (here, lax.ppermute(here, 'ch', [(i, i ^ 2) for i in range(16)]))]
    pallas_call x6, Pallas kernels: 20.1 us -> 14.7 us  [kernel_call(): pl.pallas_call(body, out_shape=tuple(outs), in_specs=[pl.BlockSpec(memory...]
    unnamed x28 -> x20, local copies, waits for them, and re-layouts: 3.57 us -> 0.04 us
    ppermute x0 -> x1, waiting for transfers between devices: none -> 1.59 us  [sum_over_channels(): return (here, lax.ppermute(here, 'ch', [(i, i ^ 2) for i in range(16)]))]
  transfers between devices with their start and end apart: 4 -> 2, of which waited for: 4 -> 2; matrix products, arithmetic and copies ran while one was open for 0% -> 0% of each run, Pallas kernels for 2% -> 1%
where the time goes in v2:
time: 110 us
  blocking collectives  41.7 us (38%)
  waiting for transfers between devices  30.1 us (27%)
  starting transfers between devices  22.3 us (20%)
  Pallas kernels  14.7 us (13%)
    all_to_all x1, waiting for transfers between devices, body(): cols = lax.all_to_all(cols, 'seq', split_axis=0, concat_axis=0, tiled=True)  28.5 us
    all_to_all x1, blocking collectives, body(): back = lax.all_to_all(back, 'seq', split_axis=0, concat_axis=0, tiled=True)  26.9 us
    all_to_all x1, blocking collectives, sum_over_channels(): lax.all_to_all(sums, 'ch', split_axis=0, concat_axis=0, axis_index_groups...  14.8 us
    pallas_call x6, Pallas kernels, kernel_call(): pl.pallas_call(body, out_shape=tuple(outs), in_specs=[pl.BlockSpec(memory...  14.7 us
    ppermute x1, starting transfers between devices, sum_over_channels(): return (here, lax.ppermute(here, 'ch', [(i, i ^ 2) for i in range(16)]))  11.3 us
    all_to_all x1, starting transfers between devices, body(): cols = lax.all_to_all(cols, 'seq', split_axis=0, concat_axis=0, tiled=True)  11.1 us
  transfers between devices with their start and end apart: 2, of which 2 were waited for; matrix products, arithmetic and copies ran while one was open for 0% of the time, Pallas kernels for 1%

profile of v2, /device:TPU:1, one launch (start us, length us, event | category | flops | bytes accessed | tf_op | source)
XLA Modules:
  0.0 109.7 jit_solution(15998114642227967127)
XLA Ops:
  0.6 0.0 copy-start.4
  0.6 0.0 copy-start.3
  0.7 2.7 %shard_map.161 = f32[8,2,256]{2,1,0:T(2,128)} custom-call(bf16[256,512]{1,0:T(8,128)(2,1)} %query.1, bf16[256,512]{1,0:T(8,128)(2,1)} %conv.1, bf16[256,512]{1,0:T(8,128)(2,1)} %cot.1, f32[1,512]{1,0:T(1,128)} %gain.3), custom_call_target="tpu_custom_call" | custom-call | bytes 804864 | tf_op jit(solution)/shard_map/pallas_call | solution.py:35
  3.4 14.8 %all_to_all.15 = f32[8,2,256]{2,1,0:T(2,128)S(1)} all-to-all(f32[8,2,256]{2,1,0:T(2,128)} %shard_map.161), channel_id=1, replica_groups={{0,1,4,5,8,9,12,13},{2,3,6,7,10,11,14,15},{16,17,20,21,24,25,28,29},{18..., dimensions={0} | all-to-all | bytes 32768 | tf_op jit(solution)/shard_map/all_to_all | solution.py:296
  18.1 0.0 copy-start.6
  18.2 0.0 copy-start
  18.2 0.0 copy-start.1
  18.2 0.0 copy-start.2
  18.2 11.3 %collective-permute-start = (f32[2,256]{1,0:T(2,128)S(1)}, f32[2,256]{1,0:T(2,128)S(1)}, u32[]{:S(2)}, u32[]{:S(2)}) collective-permute-start(f32[2,256]{1,0:T(2,128)S(1)} %reduce_sum.9.near), channel_id=1, source_target_pairs={{0,2},{1,3},{2,0},{3,1},{4,6},{5,7},{6,4},{7,5},{8,10},{9,11},{10,... | collective-permute-start | bytes 6152 | tf_op jit(solution)/shard_map/ppermute | solution.py:298
  29.5 0.0 copy-done.4
  29.5 0.0 copy-done.3
  29.5 0.3 shard_map.162.mix_cols
  29.8 1.6 %collective-permute-done.far = f32[2,256]{1,0:T(2,128)S(1)} collective-permute-done((f32[2,256]{1,0:T(2,128)S(1)}, f32[2,256]{1,0:T(2,128)S(1)}, u32[]{:S(2)}, u32[]{:S(2)}) %collective-permute-start) | collective-permute-done | bytes 2080 | tf_op jit(solution)/shard_map/ppermute | solution.py:298
  31.4 0.0 copy-done.6
  31.4 0.0 copy-done
  31.4 0.0 copy-done.1
  31.4 0.0 copy-done.2
  31.4 1.3 %shard_map.163 = (bf16[256,512]{1,0:T(8,128)(2,1)}, bf16[32,64,128]{2,1,0:T(8,128)(2,1)}, f32[1,512]{1,0:T(1,128)S(1)}) custom-call(bf16[256,512]{1,0:T(8,128)(2,1)S(1)} %copy-done, bf16[256,512]{1,0:T(8,128)(2,1)S(1)} %copy-done.1, bf16[256,512]{1,0:T(8,128)(2,1)S(1)} %copy-done.2, f32[1,512]{1,0:T(1,128)S(1)} %copy-done.6, f32[2,256]{1,0:T(2,128)S(1)} %reduce_sum.9.near, ...), custom_call_target="tpu_custom_call" | custom-call | bytes 1843200 | tf_op jit(solution)/shard_map/pallas_call | solution.py:35
  32.7 0.0 copy-start.5
  32.7 11.1 %all-to-all-start.1 = ((bf16[32,64,128]{2,1,0:T(8,128)(2,1)}), bf16[32,64,128]{2,1,0:T(8,128)(2,1)S(1)}, u32[]{:S(2)}, u32[]{:S(2)}) async-start(bf16[32,64,128]{2,1,0:T(8,128)(2,1)} %get-tuple-element.20), calls=%async_computation.1 | async-start | bytes 1048576 | tf_op jit(solution)/shard_map/all_to_all | solution.py:345
  43.8 0.0 copy-done.5
  43.8 0.6 shard_map.164.filt
  44.5 0.0 copy-start.8
  44.5 0.0 copy-start.9
  44.5 28.5 %all-to-all-done.1.cols = bf16[32,64,128]{2,1,0:T(8,128)(2,1)S(1)} async-done(((bf16[32,64,128]{2,1,0:T(8,128)(2,1)}), bf16[32,64,128]{2,1,0:T(8,128)(2,1)S(1)}, u32[]{:S(2)}, u32[]{:S(2)}) %all-to-all-start.1) | async-done | bytes 524320 | tf_op jit(solution)/shard_map/all_to_all | solution.py:345
  73.0 0.0 copy-done.8
  73.0 0.0 copy-done.9
  73.0 8.8 %shard_map.165 = (bf16[32,40,128]{2,1,0:T(8,128)(2,1)S(1)}, f32[16,8192]{1,0:T(8,128)}, f32[1,16]{1,0:T(1,128)}, f32[1,16]{1,0:T(1,128)}) custom-call(bf16[32,64,128]{2,1,0:T(8,128)(2,1)S(1)} %all-to-all-done.1.cols, bf16[32,32,128]{2,1,0:T(8,128)(2,1)S(1)} %shard_map.164.filt, f32[1,16]{1,0:T(1,128)S(1)} %copy-done.8, ...), custom_call_target="tpu_custom_call" | custom-call | flops 2147483648 | bytes 1640704 | tf_op jit(solution)/shard_map/pallas_call | solution.py:35
  81.8 0.0 copy-start.7
  81.8 26.9 %all_to_all.16.back = bf16[32,40,128]{2,1,0:T(8,128)(2,1)S(1)} all-to-all(bf16[32,40,128]{2,1,0:T(8,128)(2,1)S(1)} %get-tuple-element.22), channel_id=1, replica_groups=mesh['seq'=32,'ch'=16] {'seq'}, dimensions={0} | all-to-all | bytes 655360 | tf_op jit(solution)/shard_map/all_to_all | solution.py:349
  108.7 0.0 copy-done.7
  108.7 1.0 shard_map.166
  (1 shorter events, 0.0 us)
Async XLA Ops:
  0.6 28.8 %copy-start.4 = (bf16[256,512]{1,0:T(8,128)(2,1)S(1)}, bf16[256,512]{1,0:T(8,128)(2,1)}, u32[]{:S(2)}) copy-start(bf16[256,512]{1,0:T(8,128)(2,1)} %value.3) | copy-start | bytes 786436
  0.6 28.8 %copy-start.3 = (bf16[256,512]{1,0:T(8,128)(2,1)S(1)}, bf16[256,512]{1,0:T(8,128)(2,1)}, u32[]{:S(2)}) copy-start(bf16[256,512]{1,0:T(8,128)(2,1)} %key.3) | copy-start | bytes 786436
  18.1 13.2 %copy-start.6 = (f32[1,512]{1,0:T(1,128)S(1)}, f32[1,512]{1,0:T(1,128)}, u32[]{:S(2)}) copy-start(f32[1,512]{1,0:T(1,128)} %gain.3) | copy-start | bytes 6148
  18.2 13.2 %copy-start = (bf16[256,512]{1,0:T(8,128)(2,1)S(1)}, bf16[256,512]{1,0:T(8,128)(2,1)}, u32[]{:S(2)}) copy-start(bf16[256,512]{1,0:T(8,128)(2,1)} %query.1) | copy-start | bytes 786436
  18.2 13.2 %copy-start.1 = (bf16[256,512]{1,0:T(8,128)(2,1)S(1)}, bf16[256,512]{1,0:T(8,128)(2,1)}, u32[]{:S(2)}) copy-start(bf16[256,512]{1,0:T(8,128)(2,1)} %conv.1) | copy-start | bytes 786436
  18.2 13.2 %copy-start.2 = (bf16[256,512]{1,0:T(8,128)(2,1)S(1)}, bf16[256,512]{1,0:T(8,128)(2,1)}, u32[]{:S(2)}) copy-start(bf16[256,512]{1,0:T(8,128)(2,1)} %cot.1) | copy-start | bytes 786436
  18.2 13.2 %collective-permute-start = (f32[2,256]{1,0:T(2,128)S(1)}, f32[2,256]{1,0:T(2,128)S(1)}, u32[]{:S(2)}, u32[]{:S(2)}) collective-permute-start(f32[2,256]{1,0:T(2,128)S(1)} %reduce_sum.9.near), channel_id=1, source_target_pairs={{0,2},{1,3},{2,0},{3,1},{4,6},{5,7},{6,4},{7,5},{8,10},{9,11},{10,... | collective-permute-start | bytes 6152 | tf_op jit(solution)/shard_map/ppermute | solution.py:298
  32.7 11.1 %copy-start.5 = (f32[1,16,8192]{2,1,0:T(8,128)S(1)}, f32[1,16,8192]{2,1,0:T(8,128)}, u32[]{:S(2)}) copy-start(f32[1,16,8192]{2,1,0:T(8,128)} %param.17) | copy-start | bytes 1572868
  32.7 40.3 %all-to-all-start.1 = ((bf16[32,64,128]{2,1,0:T(8,128)(2,1)}), bf16[32,64,128]{2,1,0:T(8,128)(2,1)S(1)}, u32[]{:S(2)}, u32[]{:S(2)}) async-start(bf16[32,64,128]{2,1,0:T(8,128)(2,1)} %get-tuple-element.20), calls=%async_computation.1 | async-start | bytes 1048576 | tf_op jit(solution)/shard_map/all_to_all | solution.py:345
  44.5 28.5 %copy-start.8 = (f32[1,16]{1,0:T(1,128)S(1)}, f32[1,16]{1,0:T(1,128)}, u32[]{:S(2)}) copy-start(f32[1,16]{1,0:T(1,128)} %skip.1) | copy-start | bytes 196
  44.5 28.5 %copy-start.9 = (f32[1,16]{1,0:T(1,128)S(1)}, f32[1,16]{1,0:T(1,128)}, u32[]{:S(2)}) copy-start(f32[1,16]{1,0:T(1,128)} %col_prev.1) | copy-start | bytes 196
  81.8 26.9 %copy-start.7 = (f32[1,256]{1,0:T(1,128)S(1)}, f32[1,256]{1,0:T(1,128)}, u32[]{:S(2)}) copy-start(f32[1,256]{1,0:T(1,128)} %row_prev.1) | copy-start | bytes 3076

commit v3 on v2

--- a/solution.py
+++ b/solution.py
@@ -1,4 +1,5 @@
 import functools
+import itertools
 import math
 
 import jax
@@ -47,29 +48,32 @@
     return jax.ShapeDtypeStruct(dims, dtype)
 
 
-def token_sums(query_at, conv_at, cot_at, gain, out, query, conv, cot, sems):
-    copies = [
-        pltpu.make_async_copy(src, dst, sems.at[i])
-        for i, (src, dst) in enumerate([(query_at, query), (conv_at, conv), (cot_at, cot)])
-    ]
-    for copy in copies:
-        copy.start()
-    for copy in copies:
-        copy.wait()
-    gated = query[...].astype(F32) * conv[...].astype(F32)
-    scaled = cot[...].astype(F32) * gain[...]
-    width = gated.shape[1]
-
-    def fold(x):
-        part = sum(x[:, k : k + LANE] for k in range(0, width, LANE))
-        cols = [
-            jnp.sum(part[r : r + LANE].T, axis=0, keepdims=True) for r in range(0, part.shape[0], LANE)
-        ]
-        return jnp.concatenate(cols, axis=1)
-
-    both = jnp.concatenate([fold(gated * gated), fold(scaled * gated)], axis=0)
-    for peer in range(out.shape[0]):
-        out[peer] = both
+def token_sums(query_at, conv_at, cot_at, gain_at, out, query, conv, cot, gain, sems):
+    rows, width = query.shape
+    pairs = [(query_at, query), (conv_at, conv), (cot_at, cot)]
+    copies = []
+    gain_copy = pltpu.make_async_copy(gain_at, gain, sems.at[rows // LANE, 0])
+    gain_copy.start()
+    for r in range(rows // LANE):
+        at = pl.ds(r * LANE, LANE)
+        copies.append([pltpu.make_async_copy(x.at[at], y.at[at], sems.at[r, i]) for i, (x, y) in enumerate(pairs)])
+        for copy in copies[-1]:
+            copy.start()
+    gain_copy.wait()
+    gain_row = gain[...]
+    for r in range(rows // LANE):
+        for copy in copies[r]:
+            copy.wait()
+        at = slice(r * LANE, (r + 1) * LANE)
+        square = jnp.zeros((LANE, LANE), F32)
+        dot = jnp.zeros((LANE, LANE), F32)
+        for k in range(0, width, LANE):
+            gated = query[at, k : k + LANE].astype(F32) * conv[at, k : k + LANE].astype(F32)
+            square = square + gated * gated
+            dot = dot + cot[at, k : k + LANE].astype(F32) * gain_row[:, k : k + LANE] * gated
+        both = jnp.concatenate([jnp.sum(x.T, axis=0, keepdims=True) for x in (square, dot)], axis=0)
+        for peer in range(out.shape[0]):
+            out[peer, :, at] = both
 
 
 def mix_columns(key, value, out):
@@ -94,12 +98,36 @@
             out[n, tile * 16 : tile * 16 + 16, :] = block[:, tile * LANE : (tile + 1) * LANE]
 
 
-def token_grads(total_width, query, conv, cot, gain, near, far, mix_cols, grad_query, cols, gain_part):
+def turned_products(query, conv, cot, gain, plain, gated_q):
+    for half in range(query.shape[0] // LANE):
+        for cb in range(query.shape[1] // LANE):
+            at = (slice(half * LANE, (half + 1) * LANE), slice(cb * LANE, (cb + 1) * LANE))
+            to = (slice(cb * LANE, (cb + 1) * LANE), slice(half * LANE, (half + 1) * LANE))
+            query32 = query[at].astype(F32)
+            plain[to] = (cot[at].astype(F32) * gain[:, at[1]] * query32).T
+            gated_q[to] = (query32 * conv[at].astype(F32) * query32).T
+
+
+def token_scales(total_width, near, far):
     totals = near[...] + far[...]
-    inv_row = lax.rsqrt(totals[0:1, :] / total_width + EPS_NORM)
-    back_row = inv_row * inv_row * (totals[1:2, :] / total_width)
+    inv = lax.rsqrt(totals[0:1, :] / total_width + EPS_NORM)
+    return inv, inv * inv * (totals[1:2, :] / total_width)
+
+
+def send_columns(total_width, plain, gated_q, near, far, mix_cols, cols):
+    inv, back = token_scales(total_width, near, far)
+    cols[:, 32:64, :] = mix_cols[...]
+    for half in range(plain.shape[1] // LANE):
+        lo = slice(half * LANE, (half + 1) * LANE)
+        for d in range(cols.shape[0]):
+            at = (slice(d * 16, d * 16 + 16), lo)
+            grad = inv[:, lo] * (plain[at] - back[:, lo] * gated_q[at])
+            cols[d, half * 16 : half * 16 + 16, :] = grad.astype(BF16)
+
+
+def token_grads(total_width, query, conv, cot, gain, near, far, grad_query, gain_part):
     rows = query.shape[0]
-    cols[:, 32:64, :] = mix_cols[...]
+    inv_row, back_row = token_scales(total_width, near, far)
     both = jnp.concatenate([inv_row, back_row, jnp.zeros((6, rows), F32)], axis=0)
     for half in range(rows // LANE):
         lo = half * LANE
@@ -108,15 +136,11 @@
         back = turned[:, 1:2]
         for cb in range(query.shape[1] // LANE):
             at = (slice(lo, lo + LANE), slice(cb * LANE, (cb + 1) * LANE))
-            query32 = query[at].astype(F32)
             conv32 = conv[at].astype(F32)
             cot32 = cot[at].astype(F32)
-            gated = query32 * conv32
+            gated = query[at].astype(F32) * conv32
             grad = inv * (cot32 * gain[:, at[1]] - gated * back)
             grad_query[at] = (grad * conv32).astype(BF16)
-            block = (grad * query32).T.astype(BF16)
-            for d in range(8):
-                cols[cb * 8 + d, half * 16 : half * 16 + 16, :] = block[d * 16 : d * 16 + 16, :]
             part = jnp.sum(cot32 * gated * inv, axis=0, keepdims=True)
             if half == 0:
                 gain_part[:, at[1]] = part
@@ -158,7 +182,7 @@
                 wide_s[low, at, :] = jnp.where(lane < HALF, now[tile], later_rolled[tile])
                 wide_s[low + 1, at, :] = jnp.where(lane < HALF, now_rolled[tile], later[tile])
             now, now_rolled = later, later_rolled
-    for b in range(2):
+    for b in range(4):
         hankel[b, n_tiles * 32 : (n_tiles + 1) * 32, :] = jnp.zeros((32, LANE), BF16)
         for seg in range(segments):
             wide_c[b, seg, 0 : peers - lead, :] = jnp.zeros((peers - lead, LANE), F32)
@@ -179,6 +203,8 @@
             later = turned(k + 1)
             hankel[b, k * 32 : (k + 1) * 32, :] = jnp.where(rows_kept, now, later).astype(BF16)
             now = later
+            if k % 16 == 15:
+                yield
 
     def dots(c, b):
         cuts = 4
@@ -186,24 +212,22 @@
         for q in reversed(range(cuts)):
             rows = peers // cuts * (q + 1)
             skipped = peers - rows
-            part = None
+            left, right = [], []
             for n in range(peers // cuts * q, peers // cuts * (q + 1), 4):
-                left = []
                 for half in range(2):
                     at = n + 2 * half + 1 + skipped
                     left.append(
                         jnp.concatenate([wide_c[b, seg, at : at + rows, :] for seg in range(segments)], axis=0).astype(BF16)
                     )
-                right = []
                 for k in range(2 * n, 2 * n + 8, 2):
                     for t in (k + 1, k):
                         right.append(
                             jnp.concatenate([hankel[b, 32 * t : 32 * t + 32, :], hankel[b, 32 * t + 32 : 32 * t + 64, :]], axis=1)
                         )
-                got = jnp.dot(
-                    jnp.concatenate(left, axis=1), jnp.concatenate(right, axis=0), preferred_element_type=F32
-                )
-                part = got if part is None else part + got
+            part = jnp.dot(
+                jnp.concatenate(left, axis=1), jnp.concatenate(right, axis=0), preferred_element_type=F32
+            )
+            yield
             pieces = [part[seg * rows : (seg + 1) * rows] for seg in range(segments)]
             if total is None:
                 total = pieces
@@ -226,17 +250,19 @@
             for tile in range(2):
                 out[tile, pl.ds(c, peers, stride=chans), :] = sums[:, tile * LANE : (tile + 1) * LANE]
 
-    build(0, 0)
-
-    def pair(i, carry):
-        c = 2 * i
-        build(c + 1, 1)
-        dots(c, 0)
-        build(jnp.minimum(c + 2, chans - 1), 0)
-        dots(c + 1, 1)
+    def together(*steps):
+        for _ in itertools.zip_longest(*steps):
+            pass
+
+    together(build(0, 0), build(1, 1))
+
+    def four(i, carry):
+        c = 4 * i
+        together(build(c + 2, 2), build(c + 3, 3), dots(c, 0), dots(c + 1, 1))
+        together(build(jnp.minimum(c + 4, chans - 2), 0), build(jnp.minimum(c + 5, chans - 1), 1), dots(c + 2, 2), dots(c + 3, 3))
         return carry
 
-    lax.fori_loop(0, chans // 2, pair, 0)
+    lax.fori_loop(0, chans // 4, four, 0)
 
     diagonal = iota((chans, LANE), 0) == iota((chans, LANE), 1)
 
@@ -311,9 +337,9 @@
         [
             pltpu.VMEM((2 * peers * chans, LANE), F32),
             pltpu.VMEM((2 * STEP, (peers + 8) * chans, LANE), F32),
-            pltpu.VMEM((2, (2 * peers + 1) * 32, LANE), BF16),
-            pltpu.VMEM((2, 2 * peers, LANE), F32),
-            pltpu.VMEM((2, 2 * STEP, 2 * peers, LANE), F32),
+            pltpu.VMEM((4, (2 * peers + 1) * 32, LANE), BF16),
+            pltpu.VMEM((4, 2 * peers, LANE), F32),
+            pltpu.VMEM((4, 2 * STEP, 2 * peers, LANE), F32),
             pltpu.VMEM((2, peers * chans, LANE), F32),
             pltpu.VMEM((2, peers * chans, LANE), F32),
         ],
@@ -330,17 +356,26 @@
         token_sums,
         [shape((n_ch // 2, 2, rows), F32)],
         [query, conv, cot, norm_gain],
-        [pltpu.VMEM((rows, group), BF16)] * 3 + [pltpu.SemaphoreType.DMA((3,))],
-        in_place=(0, 1, 2),
+        [pltpu.VMEM((rows, group), BF16)] * 3
+        + [pltpu.VMEM((1, group), F32), pltpu.SemaphoreType.DMA((rows // LANE + 1, 3))],
+        in_place=(0, 1, 2, 3),
         vmem=60 << 20,
     )
     (mix_cols,) = kernel_call(mix_columns, [shape((n_seq, 32, LANE), BF16)], [key, value])
     (filt_rows,) = kernel_call(filter_rows, [shape((n_seq, 32, LANE), BF16)], [filters[0]])
     near, far = sum_over_channels(sums)
-    grad_query, cols, gain_part = kernel_call(
+    plain, gated_q = kernel_call(
+        turned_products, [shape((group, rows), F32)] * 2, [query, conv, cot, norm_gain]
+    )
+    (cols,) = kernel_call(
+        functools.partial(send_columns, group * n_ch),
+        [shape((n_seq, 64, LANE), BF16)],
+        [plain, gated_q, near, far, mix_cols],
+    )
+    grad_query, gain_part = kernel_call(
         functools.partial(token_grads, group * n_ch),
-        [shape((rows, group), BF16), shape((n_seq, 64, LANE), BF16), shape((1, group), F32)],
-        [query, conv, cot, norm_gain, near, far, mix_cols],
+        [shape((rows, group), BF16), shape((1, group), F32)],
+        [query, conv, cot, norm_gain, near, far],
     )
     cols = lax.all_to_all(cols, "seq", split_axis=0, concat_axis=0, tiled=True)
     back, grad_filt, grad_skip, col_moment = correlate_call(

time: 110 us -> 108 us (0.982)
  waiting for transfers between devices: 30.1 us -> 28.6 us
    pallas_call x6 -> x8, Pallas kernels: 14.7 us -> 13.9 us  [kernel_call(): pl.pallas_call(body, out_shape=tuple(outs), in_specs=[pl.BlockSpec(memory...]
  transfers between devices with their start and end apart: 2 -> 2, of which waited for: 2 -> 2; matrix products, arithmetic and copies ran while one was open for 0% -> 0% of each run, Pallas kernels for 1% -> 2%
where the time goes in v3:
time: 108 us; the launch traced here: 107 us
  blocking collectives  41.7 us (39%)
  waiting for transfers between devices  28.6 us (26%)
  starting transfers between devices  22.4 us (21%)
  Pallas kernels  13.9 us (13%)
    all_to_all x1, waiting for transfers between devices, body(): cols = lax.all_to_all(cols, 'seq', split_axis=0, concat_axis=0, tiled=True)  27.4 us
    all_to_all x1, blocking collectives, body(): back = lax.all_to_all(back, 'seq', split_axis=0, concat_axis=0, tiled=True)  26.9 us
    all_to_all x1, blocking collectives, sum_over_channels(): lax.all_to_all(sums, 'ch', split_axis=0, concat_axis=0, axis_index_groups...  14.8 us
    pallas_call x8, Pallas kernels, kernel_call(): pl.pallas_call(body, out_shape=tuple(outs), in_specs=[pl.BlockSpec(memory...  13.9 us
    ppermute x1, starting transfers between devices, sum_over_channels(): return (here, lax.ppermute(here, 'ch', [(i, i ^ 2) for i in range(16)]))  11.3 us
    all_to_all x1, starting transfers between devices, body(): cols = lax.all_to_all(cols, 'seq', split_axis=0, concat_axis=0, tiled=True)  11.1 us
  transfers between devices with their start and end apart: 2, of which 2 were waited for; matrix products, arithmetic and copies ran while one was open for 0% of the time, Pallas kernels for 2%

profile of v3, /device:TPU:1, one launch (start us, length us, event | category | flops | bytes accessed | tf_op | source)
XLA Modules:
  0.0 107.4 jit_solution(528583385352137481)
XLA Ops:
  0.6 0.0 copy-start
  0.6 0.0 copy-start.1
  0.7 0.0 copy-start.2
  0.7 2.1 %shard_map.161 = f32[8,2,256]{2,1,0:T(2,128)} custom-call(bf16[256,512]{1,0:T(8,128)(2,1)} %query.3, bf16[256,512]{1,0:T(8,128)(2,1)} %conv.3, bf16[256,512]{1,0:T(8,128)(2,1)} %cot.3, f32[1,512]{1,0:T(1,128)} %gain.3), custom_call_target="tpu_custom_call" | custom-call | bytes 804864 | tf_op jit(solution)/shard_map/pallas_call | solution.py:36
  2.8 14.8 %all_to_all.15 = f32[8,2,256]{2,1,0:T(2,128)S(1)} all-to-all(f32[8,2,256]{2,1,0:T(2,128)} %shard_map.161), channel_id=1, replica_groups={{0,1,4,5,8,9,12,13},{2,3,6,7,10,11,14,15},{16,17,20,21,24,25,28,29},{18..., dimensions={0} | all-to-all | bytes 32768 | tf_op jit(solution)/shard_map/all_to_all | solution.py:322
  17.6 0.0 copy-start.6
  17.6 0.0 copy-start.3
  17.6 0.0 copy-start.4
  17.6 11.3 %collective-permute-start = (f32[2,256]{1,0:T(2,128)S(1)}, f32[2,256]{1,0:T(2,128)S(1)}, u32[]{:S(2)}, u32[]{:S(2)}) collective-permute-start(f32[2,256]{1,0:T(2,128)S(1)} %reduce_sum.9.near), channel_id=1, source_target_pairs={{0,2},{1,3},{2,0},{3,1},{4,6},{5,7},{6,4},{7,5},{8,10},{9,11},{10,... | collective-permute-start | bytes 6152 | tf_op jit(solution)/shard_map/ppermute | solution.py:324
  28.9 0.0 copy-done
  28.9 0.0 copy-done.1
  28.9 0.0 copy-done.2
  28.9 0.0 copy-done.6
  28.9 0.3 shard_map.163
  29.3 0.0 copy-done.3
  29.3 0.0 copy-done.4
  29.3 0.3 shard_map.164.mix_cols
  29.6 1.2 %collective-permute-done.far = f32[2,256]{1,0:T(2,128)S(1)} collective-permute-done((f32[2,256]{1,0:T(2,128)S(1)}, f32[2,256]{1,0:T(2,128)S(1)}, u32[]{:S(2)}, u32[]{:S(2)}) %collective-permute-start) | collective-permute-done | bytes 2080 | tf_op jit(solution)/shard_map/ppermute | solution.py:324
  30.8 0.9 shard_map.165
  31.7 0.0 copy-start.5
  31.7 11.1 %all-to-all-start.1 = ((bf16[32,64,128]{2,1,0:T(8,128)(2,1)}), bf16[32,64,128]{2,1,0:T(8,128)(2,1)S(1)}, u32[]{:S(2)}, u32[]{:S(2)}) async-start(bf16[32,64,128]{2,1,0:T(8,128)(2,1)} %shard_map.165), calls=%async_computation.1 | async-start | bytes 1048576 | tf_op jit(solution)/shard_map/all_to_all | solution.py:380
  42.8 0.0 copy-done.5
  42.8 0.6 shard_map.166.filt
  43.4 1.1 %shard_map.162 = (bf16[256,512]{1,0:T(8,128)(2,1)}, f32[1,512]{1,0:T(1,128)S(1)}) custom-call(bf16[256,512]{1,0:T(8,128)(2,1)S(1)} %copy-done, bf16[256,512]{1,0:T(8,128)(2,1)S(1)} %copy-done.1, bf16[256,512]{1,0:T(8,128)(2,1)S(1)} %copy-done.2, f32[1,512]{1,0:T(1,128)S(1)} %copy-done.6, f32[2,256]{1,0:T(2,128)S(1)} %reduce_sum.9.near, ...), custom_call_target="tpu_custom_call" | custom-call | bytes 1056768 | tf_op jit(solution)/shard_map/pallas_call | solution.py:36
  44.5 0.0 copy-start.8
  44.5 0.0 copy-start.9
  44.5 27.4 %all-to-all-done.1.cols = bf16[32,64,128]{2,1,0:T(8,128)(2,1)S(1)} async-done(((bf16[32,64,128]{2,1,0:T(8,128)(2,1)}), bf16[32,64,128]{2,1,0:T(8,128)(2,1)S(1)}, u32[]{:S(2)}, u32[]{:S(2)}) %all-to-all-start.1) | async-done | bytes 524320 | tf_op jit(solution)/shard_map/all_to_all | solution.py:380
  72.0 0.0 copy-done.8
  72.0 0.0 copy-done.9
  72.0 7.5 %shard_map.167 = (bf16[32,40,128]{2,1,0:T(8,128)(2,1)S(1)}, f32[16,8192]{1,0:T(8,128)}, f32[1,16]{1,0:T(1,128)}, f32[1,16]{1,0:T(1,128)}) custom-call(bf16[32,64,128]{2,1,0:T(8,128)(2,1)S(1)} %all-to-all-done.1.cols, bf16[32,32,128]{2,1,0:T(8,128)(2,1)S(1)} %shard_map.166.filt, f32[1,16]{1,0:T(1,128)S(1)} %copy-done.8, ...), custom_call_target="tpu_custom_call" | custom-call | flops 2147483648 | bytes 1640704 | tf_op jit(solution)/shard_map/pallas_call | solution.py:36
  79.5 0.0 copy-start.7
  79.5 26.9 %all_to_all.16.back = bf16[32,40,128]{2,1,0:T(8,128)(2,1)S(1)} all-to-all(bf16[32,40,128]{2,1,0:T(8,128)(2,1)S(1)} %get-tuple-element.24), channel_id=1, replica_groups=mesh['seq'=32,'ch'=16] {'seq'}, dimensions={0} | all-to-all | bytes 655360 | tf_op jit(solution)/shard_map/all_to_all | solution.py:384
  106.4 0.0 copy-done.7
  106.4 1.0 shard_map.168
  (1 shorter events, 0.0 us)
Async XLA Ops:
  0.6 28.2 %copy-start = (bf16[256,512]{1,0:T(8,128)(2,1)S(1)}, bf16[256,512]{1,0:T(8,128)(2,1)}, u32[]{:S(2)}) copy-start(bf16[256,512]{1,0:T(8,128)(2,1)} %query.3) | copy-start | bytes 786436
  0.6 28.2 %copy-start.1 = (bf16[256,512]{1,0:T(8,128)(2,1)S(1)}, bf16[256,512]{1,0:T(8,128)(2,1)}, u32[]{:S(2)}) copy-start(bf16[256,512]{1,0:T(8,128)(2,1)} %conv.3) | copy-start | bytes 786436
  0.7 28.2 %copy-start.2 = (bf16[256,512]{1,0:T(8,128)(2,1)S(1)}, bf16[256,512]{1,0:T(8,128)(2,1)}, u32[]{:S(2)}) copy-start(bf16[256,512]{1,0:T(8,128)(2,1)} %cot.3) | copy-start | bytes 786436
  17.6 11.3 %copy-start.6 = (f32[1,512]{1,0:T(1,128)S(1)}, f32[1,512]{1,0:T(1,128)}, u32[]{:S(2)}) copy-start(f32[1,512]{1,0:T(1,128)} %gain.3) | copy-start | bytes 6148
  17.6 11.7 %copy-start.3 = (bf16[256,512]{1,0:T(8,128)(2,1)S(1)}, bf16[256,512]{1,0:T(8,128)(2,1)}, u32[]{:S(2)}) copy-start(bf16[256,512]{1,0:T(8,128)(2,1)} %key.3) | copy-start | bytes 786436
  17.6 11.7 %copy-start.4 = (bf16[256,512]{1,0:T(8,128)(2,1)S(1)}, bf16[256,512]{1,0:T(8,128)(2,1)}, u32[]{:S(2)}) copy-start(bf16[256,512]{1,0:T(8,128)(2,1)} %value.3) | copy-start | bytes 786436
  17.6 13.2 %collective-permute-start = (f32[2,256]{1,0:T(2,128)S(1)}, f32[2,256]{1,0:T(2,128)S(1)}, u32[]{:S(2)}, u32[]{:S(2)}) collective-permute-start(f32[2,256]{1,0:T(2,128)S(1)} %reduce_sum.9.near), channel_id=1, source_target_pairs={{0,2},{1,3},{2,0},{3,1},{4,6},{5,7},{6,4},{7,5},{8,10},{9,11},{10,... | collective-permute-start | bytes 6152 | tf_op jit(solution)/shard_map/ppermute | solution.py:324
  31.7 11.1 %copy-start.5 = (f32[1,16,8192]{2,1,0:T(8,128)S(1)}, f32[1,16,8192]{2,1,0:T(8,128)}, u32[]{:S(2)}) copy-start(f32[1,16,8192]{2,1,0:T(8,128)} %param.17) | copy-start | bytes 1572868
  31.7 40.3 %all-to-all-start.1 = ((bf16[32,64,128]{2,1,0:T(8,128)(2,1)}), bf16[32,64,128]{2,1,0:T(8,128)(2,1)S(1)}, u32[]{:S(2)}, u32[]{:S(2)}) async-start(bf16[32,64,128]{2,1,0:T(8,128)(2,1)} %shard_map.165), calls=%async_computation.1 | async-start | bytes 1048576 | tf_op jit(solution)/shard_map/all_to_all | solution.py:380
  44.5 27.4 %copy-start.8 = (f32[1,16]{1,0:T(1,128)S(1)}, f32[1,16]{1,0:T(1,128)}, u32[]{:S(2)}) copy-start(f32[1,16]{1,0:T(1,128)} %skip.1) | copy-start | bytes 196
  44.5 27.4 %copy-start.9 = (f32[1,16]{1,0:T(1,128)S(1)}, f32[1,16]{1,0:T(1,128)}, u32[]{:S(2)}) copy-start(f32[1,16]{1,0:T(1,128)} %col_prev.1) | copy-start | bytes 196
  79.5 26.9 %copy-start.7 = (f32[1,256]{1,0:T(1,128)S(1)}, f32[1,256]{1,0:T(1,128)}, u32[]{:S(2)}) copy-start(f32[1,256]{1,0:T(1,128)} %row_prev.1) | copy-start | bytes 3076

commit v4 on v3

--- a/solution.py
+++ b/solution.py
@@ -281,7 +281,8 @@
         for tile in range(2):
             k = 2 * d + tile
             conv = conv_s[k * chans : (k + 1) * chans, :]
-            back[d, tile * 16 : tile * 16 + 16, :] = (mix_out[tile, at, :] * scale + skip_col * conv).astype(BF16)
+            mix = (mix_out[tile, at, :] * scale + skip_col * conv).astype(BF16)
+            back[d, tile * 8 : tile * 8 + 8] = mix.reshape(8, 2, LANE)
             grad = filt_out[tile, at, :] * scale
             grad_filt[:, k * LANE : (k + 1) * LANE] = grad
             squares = grad * grad + EPS_MOMENT
@@ -289,9 +290,8 @@
             lags.append(jnp.sum(squares, axis=0, keepdims=True))
         part = gain_part[:, d // 8 * LANE : (d // 8 + 1) * LANE]
         high = part.astype(BF16).astype(F32)
-        low = (part - high).astype(BF16).astype(F32)
-        extra = jnp.concatenate(lags + [high, low, part - high - low, jnp.zeros((3, LANE), F32)], axis=0)
-        back[d, 32:40, :] = extra.astype(BF16)
+        extra = jnp.concatenate(lags + [high, part - high, jnp.zeros((12, LANE), F32)], axis=0)
+        back[d, 16:18] = extra.astype(BF16).reshape(8, 2, LANE)[0:2]
     grad_skip[...] = to_lanes(filt_out[0, (peers - 1) * chans : peers * chans, 0:1])[:, :chans]
     mean = to_lanes(jnp.sum(col_sum, axis=1, keepdims=True))[:, :chans] / (n_tiles * LANE)
     col_moment[...] = DECAY * col_prev[...] + (1.0 - DECAY) * mean
@@ -302,16 +302,16 @@
         for cb in range(key.shape[1] // LANE):
             at = (slice(half * LANE, (half + 1) * LANE), slice(cb * LANE, (cb + 1) * LANE))
             block = jnp.concatenate(
-                [back[cb * 8 + d, half * 16 : half * 16 + 16, :].astype(F32) for d in range(8)], axis=0
+                [back[cb * 8 + d, half * 8 : half * 8 + 8].reshape(16, LANE).astype(F32) for d in range(8)], axis=0
             ).T
             grad_key[at] = (block * value[at].astype(F32)).astype(BF16)
             grad_value[at] = (block * key[at].astype(F32)).astype(BF16)
-    extra = jnp.zeros((8, LANE), F32)
+    extra = jnp.zeros((4, LANE), F32)
     for d in range(back.shape[0]):
-        extra = extra + back[d, 32:40, :].astype(F32)
+        extra = extra + back[d, 16:18].reshape(4, LANE).astype(F32)
     lags = jnp.concatenate([extra[0:1], extra[1:2]], axis=1)
     row_moment[...] = DECAY * row_prev[...] + (1.0 - DECAY) * (lags / group)
-    gains = jnp.broadcast_to(extra[2:3] + extra[3:4] + extra[4:5], (8, LANE))
+    gains = jnp.broadcast_to(extra[2:3] + extra[3:4], (8, LANE))
     chans = grad_gain.shape[1]
     place = lax.rem(lax.axis_index("seq"), LANE // chans)
     grad_gain[...] = pltpu.roll(gains, lax.rem(LANE - place * chans, LANE), axis=1)[0:1, :chans]
@@ -328,7 +328,7 @@
     return kernel_call(
         functools.partial(correlations, 1.0 / math.sqrt(span)),
         [
-            shape((peers, 40, LANE), BF16),
+            shape((peers, 18, 2, LANE), BF16),
             shape((chans, span), F32),
             shape((1, chans), F32),
             shape((1, chans), F32),

time: 108 us -> 107 us (level)
  blocking collectives: 41.7 us -> 40.4 us
    all_to_all x1, blocking collectives: 26.9 us -> 25.6 us  [body(): back = lax.all_to_all(back, 'seq', split_axis=0, concat_axis=0, tiled=True)]
where the time goes in v4:
time: 107 us; the launch traced here: 106 us
  blocking collectives  40.4 us (38%)
  waiting for transfers between devices  28.6 us (27%)
  starting transfers between devices  22.4 us (21%)
  Pallas kernels  14.1 us (13%)
    all_to_all x1, waiting for transfers between devices, body(): cols = lax.all_to_all(cols, 'seq', split_axis=0, concat_axis=0, tiled=True)  27.4 us
    all_to_all x1, blocking collectives, body(): back = lax.all_to_all(back, 'seq', split_axis=0, concat_axis=0, tiled=True)  25.6 us
    all_to_all x1, blocking collectives, sum_over_channels(): lax.all_to_all(sums, 'ch', split_axis=0, concat_axis=0, axis_index_groups...  14.8 us
    pallas_call x8, Pallas kernels, kernel_call(): pl.pallas_call(body, out_shape=tuple(outs), in_specs=[pl.BlockSpec(memory...  14.1 us
    ppermute x1, starting transfers between devices, sum_over_channels(): return (here, lax.ppermute(here, 'ch', [(i, i ^ 2) for i in range(16)]))  11.3 us
    all_to_all x1, starting transfers between devices, body(): cols = lax.all_to_all(cols, 'seq', split_axis=0, concat_axis=0, tiled=True)  11.1 us
  transfers between devices with their start and end apart: 2, of which 2 were waited for; matrix products, arithmetic and copies ran while one was open for 0% of the time, Pallas kernels for 2%

profile of v4, /device:TPU:1, one launch (start us, length us, event | category | flops | bytes accessed | tf_op | source)
XLA Modules:
  0.0 106.2 jit_solution(14627974297875381441)
XLA Ops:
  0.6 0.0 copy-start
  0.6 0.0 copy-start.1
  0.7 0.0 copy-start.2
  0.7 2.1 %shard_map.161 = f32[8,2,256]{2,1,0:T(2,128)} custom-call(bf16[256,512]{1,0:T(8,128)(2,1)} %query.3, bf16[256,512]{1,0:T(8,128)(2,1)} %conv.3, bf16[256,512]{1,0:T(8,128)(2,1)} %cot.3, f32[1,512]{1,0:T(1,128)} %gain.3), custom_call_target="tpu_custom_call" | custom-call | bytes 804864 | tf_op jit(solution)/shard_map/pallas_call | solution.py:36
  2.8 14.8 %all_to_all.15 = f32[8,2,256]{2,1,0:T(2,128)S(1)} all-to-all(f32[8,2,256]{2,1,0:T(2,128)} %shard_map.161), channel_id=1, replica_groups={{0,1,4,5,8,9,12,13},{2,3,6,7,10,11,14,15},{16,17,20,21,24,25,28,29},{18..., dimensions={0} | all-to-all | bytes 32768 | tf_op jit(solution)/shard_map/all_to_all | solution.py:322
  17.6 0.0 copy-start.6
  17.6 0.0 copy-start.3
  17.6 0.0 copy-start.4
  17.6 11.3 %collective-permute-start = (f32[2,256]{1,0:T(2,128)S(1)}, f32[2,256]{1,0:T(2,128)S(1)}, u32[]{:S(2)}, u32[]{:S(2)}) collective-permute-start(f32[2,256]{1,0:T(2,128)S(1)} %reduce_sum.9.near), channel_id=1, source_target_pairs={{0,2},{1,3},{2,0},{3,1},{4,6},{5,7},{6,4},{7,5},{8,10},{9,11},{10,... | collective-permute-start | bytes 6152 | tf_op jit(solution)/shard_map/ppermute | solution.py:324
  28.9 0.0 copy-done
  28.9 0.0 copy-done.1
  28.9 0.0 copy-done.2
  28.9 0.0 copy-done.6
  28.9 0.3 shard_map.163
  29.3 0.0 copy-done.3
  29.3 0.0 copy-done.4
  29.3 0.3 shard_map.164.mix_cols
  29.6 1.2 %collective-permute-done.far = f32[2,256]{1,0:T(2,128)S(1)} collective-permute-done((f32[2,256]{1,0:T(2,128)S(1)}, f32[2,256]{1,0:T(2,128)S(1)}, u32[]{:S(2)}, u32[]{:S(2)}) %collective-permute-start) | collective-permute-done | bytes 2080 | tf_op jit(solution)/shard_map/ppermute | solution.py:324
  30.8 0.9 shard_map.165
  31.7 0.0 copy-start.5
  31.7 11.1 %all-to-all-start.1 = ((bf16[32,64,128]{2,1,0:T(8,128)(2,1)}), bf16[32,64,128]{2,1,0:T(8,128)(2,1)S(1)}, u32[]{:S(2)}, u32[]{:S(2)}) async-start(bf16[32,64,128]{2,1,0:T(8,128)(2,1)} %shard_map.165), calls=%async_computation.1 | async-start | bytes 1048576 | tf_op jit(solution)/shard_map/all_to_all | solution.py:380
  42.8 0.0 copy-done.5
  42.8 0.6 shard_map.166.filt
  43.4 1.1 %shard_map.162 = (bf16[256,512]{1,0:T(8,128)(2,1)}, f32[1,512]{1,0:T(1,128)S(1)}) custom-call(bf16[256,512]{1,0:T(8,128)(2,1)S(1)} %copy-done, bf16[256,512]{1,0:T(8,128)(2,1)S(1)} %copy-done.1, bf16[256,512]{1,0:T(8,128)(2,1)S(1)} %copy-done.2, f32[1,512]{1,0:T(1,128)S(1)} %copy-done.6, f32[2,256]{1,0:T(2,128)S(1)} %reduce_sum.9.near, ...), custom_call_target="tpu_custom_call" | custom-call | bytes 1056768 | tf_op jit(solution)/shard_map/pallas_call | solution.py:36
  44.5 0.0 copy-start.8
  44.5 0.0 copy-start.9
  44.5 27.4 %all-to-all-done.1.cols = bf16[32,64,128]{2,1,0:T(8,128)(2,1)S(1)} async-done(((bf16[32,64,128]{2,1,0:T(8,128)(2,1)}), bf16[32,64,128]{2,1,0:T(8,128)(2,1)S(1)}, u32[]{:S(2)}, u32[]{:S(2)}) %all-to-all-start.1) | async-done | bytes 524320 | tf_op jit(solution)/shard_map/all_to_all | solution.py:380
  72.0 0.0 copy-done.8
  72.0 0.0 copy-done.9
  72.0 7.6 %shard_map.167 = (bf16[32,18,2,128]{3,2,1,0:T(2,128)(2,1)S(1)}, f32[16,8192]{1,0:T(8,128)}, f32[1,16]{1,0:T(1,128)}, f32[1,16]{1,0:T(1,128)}) custom-call(bf16[32,64,128]{2,1,0:T(8,128)(2,1)S(1)} %all-to-all-done.1.cols, bf16[32,32,128]{2,1,0:T(8,128)(2,1)S(1)} %shard_map.166.filt, f32[1,16]{1,0:T(1,128)S(1)} %copy-done.8, ...), custom_call_target="tpu_custom_call" | custom-call | flops 2147483648 | bytes 1607936 | tf_op jit(solution)/shard_map/pallas_call | solution.py:36
  79.6 0.0 copy-start.7
  79.6 25.6 %all_to_all.16.back = bf16[32,18,2,128]{3,2,1,0:T(2,128)(2,1)S(1)} all-to-all(bf16[32,18,2,128]{3,2,1,0:T(2,128)(2,1)S(1)} %get-tuple-element.24), channel_id=1, replica_groups=mesh['seq'=32,'ch'=16] {'seq'}, dimensions={0} | all-to-all | bytes 589824 | tf_op jit(solution)/shard_map/all_to_all | solution.py:384
  105.2 0.0 copy-done.7
  105.2 1.1 %shard_map.168 = (bf16[256,512]{1,0:T(8,128)(2,1)}, bf16[256,512]{1,0:T(8,128)(2,1)}, f32[1,256]{1,0:T(1,128)}, f32[1,16]{1,0:T(1,128)}) custom-call(bf16[32,18,2,128]{3,2,1,0:T(2,128)(2,1)S(1)} %all_to_all.16.back, bf16[256,512]{1,0:T(8,128)(2,1)S(1)} %copy-done.3, bf16[256,512]{1,0:T(8,128)(2,1)S(1)} %copy-done.4, f32[1,256]{1,0:T(1,128)S(1)} %copy-done.7), custom_call_target="tpu_custom_call" | custom-call | bytes 1345600 | tf_op jit(solution)/shard_map/pallas_call | solution.py:36
  (1 shorter events, 0.0 us)
Async XLA Ops:
  0.6 28.2 %copy-start = (bf16[256,512]{1,0:T(8,128)(2,1)S(1)}, bf16[256,512]{1,0:T(8,128)(2,1)}, u32[]{:S(2)}) copy-start(bf16[256,512]{1,0:T(8,128)(2,1)} %query.3) | copy-start | bytes 786436
  0.6 28.2 %copy-start.1 = (bf16[256,512]{1,0:T(8,128)(2,1)S(1)}, bf16[256,512]{1,0:T(8,128)(2,1)}, u32[]{:S(2)}) copy-start(bf16[256,512]{1,0:T(8,128)(2,1)} %conv.3) | copy-start | bytes 786436
  0.7 28.2 %copy-start.2 = (bf16[256,512]{1,0:T(8,128)(2,1)S(1)}, bf16[256,512]{1,0:T(8,128)(2,1)}, u32[]{:S(2)}) copy-start(bf16[256,512]{1,0:T(8,128)(2,1)} %cot.3) | copy-start | bytes 786436
  17.6 11.3 %copy-start.6 = (f32[1,512]{1,0:T(1,128)S(1)}, f32[1,512]{1,0:T(1,128)}, u32[]{:S(2)}) copy-start(f32[1,512]{1,0:T(1,128)} %gain.3) | copy-start | bytes 6148
  17.6 11.7 %copy-start.3 = (bf16[256,512]{1,0:T(8,128)(2,1)S(1)}, bf16[256,512]{1,0:T(8,128)(2,1)}, u32[]{:S(2)}) copy-start(bf16[256,512]{1,0:T(8,128)(2,1)} %key.3) | copy-start | bytes 786436
  17.6 11.7 %copy-start.4 = (bf16[256,512]{1,0:T(8,128)(2,1)S(1)}, bf16[256,512]{1,0:T(8,128)(2,1)}, u32[]{:S(2)}) copy-start(bf16[256,512]{1,0:T(8,128)(2,1)} %value.3) | copy-start | bytes 786436
  17.6 13.2 %collective-permute-start = (f32[2,256]{1,0:T(2,128)S(1)}, f32[2,256]{1,0:T(2,128)S(1)}, u32[]{:S(2)}, u32[]{:S(2)}) collective-permute-start(f32[2,256]{1,0:T(2,128)S(1)} %reduce_sum.9.near), channel_id=1, source_target_pairs={{0,2},{1,3},{2,0},{3,1},{4,6},{5,7},{6,4},{7,5},{8,10},{9,11},{10,... | collective-permute-start | bytes 6152 | tf_op jit(solution)/shard_map/ppermute | solution.py:324
  31.7 11.1 %copy-start.5 = (f32[1,16,8192]{2,1,0:T(8,128)S(1)}, f32[1,16,8192]{2,1,0:T(8,128)}, u32[]{:S(2)}) copy-start(f32[1,16,8192]{2,1,0:T(8,128)} %param.17) | copy-start | bytes 1572868
  31.7 40.3 %all-to-all-start.1 = ((bf16[32,64,128]{2,1,0:T(8,128)(2,1)}), bf16[32,64,128]{2,1,0:T(8,128)(2,1)S(1)}, u32[]{:S(2)}, u32[]{:S(2)}) async-start(bf16[32,64,128]{2,1,0:T(8,128)(2,1)} %shard_map.165), calls=%async_computation.1 | async-start | bytes 1048576 | tf_op jit(solution)/shard_map/all_to_all | solution.py:380
  44.5 27.4 %copy-start.8 = (f32[1,16]{1,0:T(1,128)S(1)}, f32[1,16]{1,0:T(1,128)}, u32[]{:S(2)}) copy-start(f32[1,16]{1,0:T(1,128)} %skip.1) | copy-start | bytes 196
  44.5 27.4 %copy-start.9 = (f32[1,16]{1,0:T(1,128)S(1)}, f32[1,16]{1,0:T(1,128)}, u32[]{:S(2)}) copy-start(f32[1,16]{1,0:T(1,128)} %col_prev.1) | copy-start | bytes 196
  79.6 25.6 %copy-start.7 = (f32[1,256]{1,0:T(1,128)S(1)}, f32[1,256]{1,0:T(1,128)}, u32[]{:S(2)}) copy-start(f32[1,256]{1,0:T(1,128)} %row_prev.1) | copy-start | bytes 3076

commit v5 on v4

--- a/solution.py
+++ b/solution.py
@@ -21,6 +21,7 @@
     return lax.broadcasted_iota(jnp.int32, shape, axis)
 
 
+PITCH = 17
 STEP = 4
 HALF = 64
 
@@ -167,16 +168,18 @@
         return [ref[n, first + tile * 16 : first + tile * 16 + 16, :].astype(F32) for tile in range(2)]
 
     for d in range(peers):
-        conv_s[d * 32 : d * 32 + 32, :] = cols[d, 0:32, :].astype(F32)
+        for tile in range(2):
+            at = PITCH * (2 * d + tile)
+            conv_s[at : at + chans, :] = cols[d, tile * 16 : tile * 16 + 16, :].astype(F32)
     for which, (ref, first) in enumerate([(filt, 0), (cols, 32)]):
         for r in range(STEP):
-            wide_s[which * STEP + r, 0 : lead * chans, :] = jnp.zeros((lead * chans, LANE), F32)
+            wide_s[which * STEP + r, 0 : lead * PITCH, :] = jnp.zeros((lead * PITCH, LANE), F32)
         now = residues(ref, -1, first)
         now_rolled = now
         for n in range(-1, peers - 1):
             later = residues(ref, n + 1, first)
             later_rolled = [pltpu.roll(x, HALF, axis=1) for x in later]
-            at = slice((lead + n) * chans, (lead + n + 1) * chans)
+            at = slice((lead + n) * PITCH, (lead + n) * PITCH + chans)
             for tile in range(2):
                 low = which * STEP + 2 * tile
                 wide_s[low, at, :] = jnp.where(lane < HALF, now[tile], later_rolled[tile])
@@ -188,9 +191,9 @@
             wide_c[b, seg, 0 : peers - lead, :] = jnp.zeros((peers - lead, LANE), F32)
 
     def build(c, b):
-        conv_c[b] = conv_s[pl.ds(c, n_tiles, stride=chans), :]
+        conv_c[b] = conv_s[pl.ds(c, n_tiles, stride=PITCH), :]
         for seg in range(segments):
-            wide_c[b, seg, peers - lead : 2 * peers, :] = wide_s[seg, pl.ds(c, peers + lead, stride=chans), :]
+            wide_c[b, seg, peers - lead : 2 * peers, :] = wide_s[seg, pl.ds(c, peers + lead, stride=PITCH), :]
 
         def turned(k):
             if k == n_tiles:
@@ -232,8 +235,9 @@
             if total is None:
                 total = pieces
             else:
-                blank = jnp.zeros((skipped, 2 * LANE), F32)
-                total = [x + jnp.concatenate([blank, y], axis=0) for x, y in zip(total, pieces)]
+                total = [
+                    jnp.concatenate([x[:skipped], x[skipped:] + y], axis=0) for x, y in zip(total, pieces)
+                ]
 
         inner = iota((peers, LANE), 1) < LANE - 1
         top = jnp.zeros((1, LANE), F32)
@@ -248,7 +252,7 @@
             for r in reversed(range(STEP - 1)):
                 sums = total[which * STEP + r] + later_by_one(sums)
             for tile in range(2):
-                out[tile, pl.ds(c, peers, stride=chans), :] = sums[:, tile * LANE : (tile + 1) * LANE]
+                out[tile, pl.ds(c, peers, stride=PITCH), :] = sums[:, tile * LANE : (tile + 1) * LANE]
 
     def together(*steps):
         for _ in itertools.zip_longest(*steps):
@@ -276,11 +280,11 @@
     )
     col_sum = jnp.zeros((chans, LANE), F32)
     for d in range(peers):
-        at = slice((peers - 1 - d) * chans, (peers - d) * chans)
+        at = slice((peers - 1 - d) * PITCH, (peers - 1 - d) * PITCH + chans)
         lags = []
         for tile in range(2):
             k = 2 * d + tile
-            conv = conv_s[k * chans : (k + 1) * chans, :]
+            conv = conv_s[PITCH * k : PITCH * k + chans, :]
             mix = (mix_out[tile, at, :] * scale + skip_col * conv).astype(BF16)
             back[d, tile * 8 : tile * 8 + 8] = mix.reshape(8, 2, LANE)
             grad = filt_out[tile, at, :] * scale
@@ -292,7 +296,7 @@
         high = part.astype(BF16).astype(F32)
         extra = jnp.concatenate(lags + [high, part - high, jnp.zeros((12, LANE), F32)], axis=0)
         back[d, 16:18] = extra.astype(BF16).reshape(8, 2, LANE)[0:2]
-    grad_skip[...] = to_lanes(filt_out[0, (peers - 1) * chans : peers * chans, 0:1])[:, :chans]
+    grad_skip[...] = to_lanes(filt_out[0, (peers - 1) * PITCH : (peers - 1) * PITCH + chans, 0:1])[:, :chans]
     mean = to_lanes(jnp.sum(col_sum, axis=1, keepdims=True))[:, :chans] / (n_tiles * LANE)
     col_moment[...] = DECAY * col_prev[...] + (1.0 - DECAY) * mean
 
@@ -335,13 +339,13 @@
         ],
         args,
         [
-            pltpu.VMEM((2 * peers * chans, LANE), F32),
-            pltpu.VMEM((2 * STEP, (peers + 8) * chans, LANE), F32),
+            pltpu.VMEM((2 * peers * PITCH, LANE), F32),
+            pltpu.VMEM((2 * STEP, (peers + 8) * PITCH, LANE), F32),
             pltpu.VMEM((4, (2 * peers + 1) * 32, LANE), BF16),
             pltpu.VMEM((4, 2 * peers, LANE), F32),
             pltpu.VMEM((4, 2 * STEP, 2 * peers, LANE), F32),
-            pltpu.VMEM((2, peers * chans, LANE), F32),
-            pltpu.VMEM((2, peers * chans, LANE), F32),
+            pltpu.VMEM((2, peers * PITCH, LANE), F32),
+            pltpu.VMEM((2, peers * PITCH, LANE), F32),
         ],
         flops=2 * chans * span * span,
         vmem=40 << 20,

time: 107 us -> 106 us (level)
  no operation moved by 1% of the time
where the time goes in v5:
time: 106 us; the launch traced here: 105 us
  blocking collectives  40.4 us (38%)
  waiting for transfers between devices  28.6 us (27%)
  starting transfers between devices  22.4 us (21%)
  Pallas kernels  13.1 us (12%)
    all_to_all x1, waiting for transfers between devices, body(): cols = lax.all_to_all(cols, 'seq', split_axis=0, concat_axis=0, tiled=True)  27.4 us
    all_to_all x1, blocking collectives, body(): back = lax.all_to_all(back, 'seq', split_axis=0, concat_axis=0, tiled=True)  25.6 us
    all_to_all x1, blocking collectives, sum_over_channels(): lax.all_to_all(sums, 'ch', split_axis=0, concat_axis=0, axis_index_groups...  14.8 us
    pallas_call x8, Pallas kernels, kernel_call(): pl.pallas_call(body, out_shape=tuple(outs), in_specs=[pl.BlockSpec(memory...  13.1 us
    ppermute x1, starting transfers between devices, sum_over_channels(): return (here, lax.ppermute(here, 'ch', [(i, i ^ 2) for i in range(16)]))  11.3 us
    all_to_all x1, starting transfers between devices, body(): cols = lax.all_to_all(cols, 'seq', split_axis=0, concat_axis=0, tiled=True)  11.1 us
  transfers between devices with their start and end apart: 2, of which 2 were waited for; matrix products, arithmetic and copies ran while one was open for 0% of the time, Pallas kernels for 2%

profile of v5, /device:TPU:1, one launch (start us, length us, event | category | flops | bytes accessed | tf_op | source)
XLA Modules:
  0.0 105.3 jit_solution(3555821797223742519)
XLA Ops:
  0.6 0.0 copy-start
  0.6 0.0 copy-start.1
  0.7 0.0 copy-start.2
  0.7 2.1 %shard_map.161 = f32[8,2,256]{2,1,0:T(2,128)} custom-call(bf16[256,512]{1,0:T(8,128)(2,1)} %query.3, bf16[256,512]{1,0:T(8,128)(2,1)} %conv.3, bf16[256,512]{1,0:T(8,128)(2,1)} %cot.3, f32[1,512]{1,0:T(1,128)} %gain.3), custom_call_target="tpu_custom_call" | custom-call | bytes 804864 | tf_op jit(solution)/shard_map/pallas_call | solution.py:37
  2.8 14.8 %all_to_all.15 = f32[8,2,256]{2,1,0:T(2,128)S(1)} all-to-all(f32[8,2,256]{2,1,0:T(2,128)} %shard_map.161), channel_id=1, replica_groups={{0,1,4,5,8,9,12,13},{2,3,6,7,10,11,14,15},{16,17,20,21,24,25,28,29},{18..., dimensions={0} | all-to-all | bytes 32768 | tf_op jit(solution)/shard_map/all_to_all | solution.py:326
  17.6 0.0 copy-start.6
  17.6 0.0 copy-start.3
  17.6 0.0 copy-start.4
  17.6 11.3 %collective-permute-start = (f32[2,256]{1,0:T(2,128)S(1)}, f32[2,256]{1,0:T(2,128)S(1)}, u32[]{:S(2)}, u32[]{:S(2)}) collective-permute-start(f32[2,256]{1,0:T(2,128)S(1)} %reduce_sum.9.near), channel_id=1, source_target_pairs={{0,2},{1,3},{2,0},{3,1},{4,6},{5,7},{6,4},{7,5},{8,10},{9,11},{10,... | collective-permute-start | bytes 6152 | tf_op jit(solution)/shard_map/ppermute | solution.py:328
  28.9 0.0 copy-done
  28.9 0.0 copy-done.1
  28.9 0.0 copy-done.2
  28.9 0.0 copy-done.6
  28.9 0.3 shard_map.163
  29.3 0.0 copy-done.3
  29.3 0.0 copy-done.4
  29.3 0.3 shard_map.164.mix_cols
  29.6 1.2 %collective-permute-done.far = f32[2,256]{1,0:T(2,128)S(1)} collective-permute-done((f32[2,256]{1,0:T(2,128)S(1)}, f32[2,256]{1,0:T(2,128)S(1)}, u32[]{:S(2)}, u32[]{:S(2)}) %collective-permute-start) | collective-permute-done | bytes 2080 | tf_op jit(solution)/shard_map/ppermute | solution.py:328
  30.8 0.9 shard_map.165
  31.7 0.0 copy-start.5
  31.7 11.1 %all-to-all-start.1 = ((bf16[32,64,128]{2,1,0:T(8,128)(2,1)}), bf16[32,64,128]{2,1,0:T(8,128)(2,1)S(1)}, u32[]{:S(2)}, u32[]{:S(2)}) async-start(bf16[32,64,128]{2,1,0:T(8,128)(2,1)} %shard_map.165), calls=%async_computation.1 | async-start | bytes 1048576 | tf_op jit(solution)/shard_map/all_to_all | solution.py:384
  42.8 0.0 copy-done.5
  42.8 0.6 shard_map.166.filt
  43.4 1.1 %shard_map.162 = (bf16[256,512]{1,0:T(8,128)(2,1)}, f32[1,512]{1,0:T(1,128)S(1)}) custom-call(bf16[256,512]{1,0:T(8,128)(2,1)S(1)} %copy-done, bf16[256,512]{1,0:T(8,128)(2,1)S(1)} %copy-done.1, bf16[256,512]{1,0:T(8,128)(2,1)S(1)} %copy-done.2, f32[1,512]{1,0:T(1,128)S(1)} %copy-done.6, f32[2,256]{1,0:T(2,128)S(1)} %reduce_sum.9.near, ...), custom_call_target="tpu_custom_call" | custom-call | bytes 1056768 | tf_op jit(solution)/shard_map/pallas_call | solution.py:37
  44.5 0.0 copy-start.8
  44.5 0.0 copy-start.9
  44.5 27.4 %all-to-all-done.1.cols = bf16[32,64,128]{2,1,0:T(8,128)(2,1)S(1)} async-done(((bf16[32,64,128]{2,1,0:T(8,128)(2,1)}), bf16[32,64,128]{2,1,0:T(8,128)(2,1)S(1)}, u32[]{:S(2)}, u32[]{:S(2)}) %all-to-all-start.1) | async-done | bytes 524320 | tf_op jit(solution)/shard_map/all_to_all | solution.py:384
  72.0 0.0 copy-done.8
  72.0 0.0 copy-done.9
  72.0 6.7 %shard_map.167 = (bf16[32,18,2,128]{3,2,1,0:T(2,128)(2,1)S(1)}, f32[16,8192]{1,0:T(8,128)}, f32[1,16]{1,0:T(1,128)}, f32[1,16]{1,0:T(1,128)}) custom-call(bf16[32,64,128]{2,1,0:T(8,128)(2,1)S(1)} %all-to-all-done.1.cols, bf16[32,32,128]{2,1,0:T(8,128)(2,1)S(1)} %shard_map.166.filt, f32[1,16]{1,0:T(1,128)S(1)} %copy-done.8, ...), custom_call_target="tpu_custom_call" | custom-call | flops 2147483648 | bytes 1607936 | tf_op jit(solution)/shard_map/pallas_call | solution.py:37
  78.7 0.0 copy-start.7
  78.7 25.6 %all_to_all.16.back = bf16[32,18,2,128]{3,2,1,0:T(2,128)(2,1)S(1)} all-to-all(bf16[32,18,2,128]{3,2,1,0:T(2,128)(2,1)S(1)} %get-tuple-element.24), channel_id=1, replica_groups=mesh['seq'=32,'ch'=16] {'seq'}, dimensions={0} | all-to-all | bytes 589824 | tf_op jit(solution)/shard_map/all_to_all | solution.py:388
  104.3 0.0 copy-done.7
  104.3 1.1 %shard_map.168 = (bf16[256,512]{1,0:T(8,128)(2,1)}, bf16[256,512]{1,0:T(8,128)(2,1)}, f32[1,256]{1,0:T(1,128)}, f32[1,16]{1,0:T(1,128)}) custom-call(bf16[32,18,2,128]{3,2,1,0:T(2,128)(2,1)S(1)} %all_to_all.16.back, bf16[256,512]{1,0:T(8,128)(2,1)S(1)} %copy-done.3, bf16[256,512]{1,0:T(8,128)(2,1)S(1)} %copy-done.4, f32[1,256]{1,0:T(1,128)S(1)} %copy-done.7), custom_call_target="tpu_custom_call" | custom-call | bytes 1345600 | tf_op jit(solution)/shard_map/pallas_call | solution.py:37
  (1 shorter events, 0.0 us)
Async XLA Ops:
  0.6 28.2 %copy-start = (bf16[256,512]{1,0:T(8,128)(2,1)S(1)}, bf16[256,512]{1,0:T(8,128)(2,1)}, u32[]{:S(2)}) copy-start(bf16[256,512]{1,0:T(8,128)(2,1)} %query.3) | copy-start | bytes 786436
  0.6 28.2 %copy-start.1 = (bf16[256,512]{1,0:T(8,128)(2,1)S(1)}, bf16[256,512]{1,0:T(8,128)(2,1)}, u32[]{:S(2)}) copy-start(bf16[256,512]{1,0:T(8,128)(2,1)} %conv.3) | copy-start | bytes 786436
  0.7 28.2 %copy-start.2 = (bf16[256,512]{1,0:T(8,128)(2,1)S(1)}, bf16[256,512]{1,0:T(8,128)(2,1)}, u32[]{:S(2)}) copy-start(bf16[256,512]{1,0:T(8,128)(2,1)} %cot.3) | copy-start | bytes 786436
  17.6 11.3 %copy-start.6 = (f32[1,512]{1,0:T(1,128)S(1)}, f32[1,512]{1,0:T(1,128)}, u32[]{:S(2)}) copy-start(f32[1,512]{1,0:T(1,128)} %gain.3) | copy-start | bytes 6148
  17.6 11.7 %copy-start.3 = (bf16[256,512]{1,0:T(8,128)(2,1)S(1)}, bf16[256,512]{1,0:T(8,128)(2,1)}, u32[]{:S(2)}) copy-start(bf16[256,512]{1,0:T(8,128)(2,1)} %key.3) | copy-start | bytes 786436
  17.6 11.7 %copy-start.4 = (bf16[256,512]{1,0:T(8,128)(2,1)S(1)}, bf16[256,512]{1,0:T(8,128)(2,1)}, u32[]{:S(2)}) copy-start(bf16[256,512]{1,0:T(8,128)(2,1)} %value.3) | copy-start | bytes 786436
  17.6 13.2 %collective-permute-start = (f32[2,256]{1,0:T(2,128)S(1)}, f32[2,256]{1,0:T(2,128)S(1)}, u32[]{:S(2)}, u32[]{:S(2)}) collective-permute-start(f32[2,256]{1,0:T(2,128)S(1)} %reduce_sum.9.near), channel_id=1, source_target_pairs={{0,2},{1,3},{2,0},{3,1},{4,6},{5,7},{6,4},{7,5},{8,10},{9,11},{10,... | collective-permute-start | bytes 6152 | tf_op jit(solution)/shard_map/ppermute | solution.py:328
  31.7 11.1 %copy-start.5 = (f32[1,16,8192]{2,1,0:T(8,128)S(1)}, f32[1,16,8192]{2,1,0:T(8,128)}, u32[]{:S(2)}) copy-start(f32[1,16,8192]{2,1,0:T(8,128)} %param.17) | copy-start | bytes 1572868
  31.7 40.3 %all-to-all-start.1 = ((bf16[32,64,128]{2,1,0:T(8,128)(2,1)}), bf16[32,64,128]{2,1,0:T(8,128)(2,1)S(1)}, u32[]{:S(2)}, u32[]{:S(2)}) async-start(bf16[32,64,128]{2,1,0:T(8,128)(2,1)} %shard_map.165), calls=%async_computation.1 | async-start | bytes 1048576 | tf_op jit(solution)/shard_map/all_to_all | solution.py:384
  44.5 27.4 %copy-start.8 = (f32[1,16]{1,0:T(1,128)S(1)}, f32[1,16]{1,0:T(1,128)}, u32[]{:S(2)}) copy-start(f32[1,16]{1,0:T(1,128)} %skip.1) | copy-start | bytes 196
  44.5 27.4 %copy-start.9 = (f32[1,16]{1,0:T(1,128)S(1)}, f32[1,16]{1,0:T(1,128)}, u32[]{:S(2)}) copy-start(f32[1,16]{1,0:T(1,128)} %col_prev.1) | copy-start | bytes 196
  78.7 25.6 %copy-start.7 = (f32[1,256]{1,0:T(1,128)S(1)}, f32[1,256]{1,0:T(1,128)}, u32[]{:S(2)}) copy-start(f32[1,256]{1,0:T(1,128)} %row_prev.1) | copy-start | bytes 3076

commit v6 on v5

--- a/solution.py
+++ b/solution.py
@@ -339,13 +339,13 @@
         ],
         args,
         [
-            pltpu.VMEM((2 * peers * PITCH, LANE), F32),
-            pltpu.VMEM((2 * STEP, (peers + 8) * PITCH, LANE), F32),
+            pltpu.VMEM(((2 * peers + 1) * PITCH, LANE), F32),
+            pltpu.VMEM((2 * STEP, (peers + 9) * PITCH, LANE), F32),
             pltpu.VMEM((4, (2 * peers + 1) * 32, LANE), BF16),
             pltpu.VMEM((4, 2 * peers, LANE), F32),
             pltpu.VMEM((4, 2 * STEP, 2 * peers, LANE), F32),
-            pltpu.VMEM((2, peers * PITCH, LANE), F32),
-            pltpu.VMEM((2, peers * PITCH, LANE), F32),
+            pltpu.VMEM((2, (peers + 1) * PITCH, LANE), F32),
+            pltpu.VMEM((2, (peers + 1) * PITCH, LANE), F32),
         ],
         flops=2 * chans * span * span,
         vmem=40 << 20,

time: 106 us -> 106 us (level)
  no operation moved by 1% of the time
where the time goes in v6:
time: 106 us; the launch traced here: 105 us
  blocking collectives  40.4 us (38%)
  waiting for transfers between devices  28.6 us (27%)
  starting transfers between devices  22.4 us (21%)
  Pallas kernels  13.2 us (12%)
    all_to_all x1, waiting for transfers between devices, body(): cols = lax.all_to_all(cols, 'seq', split_axis=0, concat_axis=0, tiled=True)  27.4 us
    all_to_all x1, blocking collectives, body(): back = lax.all_to_all(back, 'seq', split_axis=0, concat_axis=0, tiled=True)  25.6 us
    all_to_all x1, blocking collectives, sum_over_channels(): lax.all_to_all(sums, 'ch', split_axis=0, concat_axis=0, axis_index_groups...  14.8 us
    pallas_call x8, Pallas kernels, kernel_call(): pl.pallas_call(body, out_shape=tuple(outs), in_specs=[pl.BlockSpec(memory...  13.2 us
    ppermute x1, starting transfers between devices, sum_over_channels(): return (here, lax.ppermute(here, 'ch', [(i, i ^ 2) for i in range(16)]))  11.3 us
    all_to_all x1, starting transfers between devices, body(): cols = lax.all_to_all(cols, 'seq', split_axis=0, concat_axis=0, tiled=True)  11.1 us
  transfers between devices with their start and end apart: 2, of which 2 were waited for; matrix products, arithmetic and copies ran while one was open for 0% of the time, Pallas kernels for 2%

profile of v6, /device:TPU:1, one launch (start us, length us, event | category | flops | bytes accessed | tf_op | source)
XLA Modules:
  0.0 105.4 jit_solution(2351513495838744114)
XLA Ops:
  0.6 0.0 copy-start
  0.6 0.0 copy-start.1
  0.7 0.0 copy-start.2
  0.7 2.1 %shard_map.161 = f32[8,2,256]{2,1,0:T(2,128)} custom-call(bf16[256,512]{1,0:T(8,128)(2,1)} %query.3, bf16[256,512]{1,0:T(8,128)(2,1)} %conv.3, bf16[256,512]{1,0:T(8,128)(2,1)} %cot.3, f32[1,512]{1,0:T(1,128)} %gain.3), custom_call_target="tpu_custom_call" | custom-call | bytes 804864 | tf_op jit(solution)/shard_map/pallas_call | solution.py:37
  2.8 14.8 %all_to_all.15 = f32[8,2,256]{2,1,0:T(2,128)S(1)} all-to-all(f32[8,2,256]{2,1,0:T(2,128)} %shard_map.161), channel_id=1, replica_groups={{0,1,4,5,8,9,12,13},{2,3,6,7,10,11,14,15},{16,17,20,21,24,25,28,29},{18..., dimensions={0} | all-to-all | bytes 32768 | tf_op jit(solution)/shard_map/all_to_all | solution.py:326
  17.6 0.0 copy-start.6
  17.6 0.0 copy-start.3
  17.6 0.0 copy-start.4
  17.6 11.3 %collective-permute-start = (f32[2,256]{1,0:T(2,128)S(1)}, f32[2,256]{1,0:T(2,128)S(1)}, u32[]{:S(2)}, u32[]{:S(2)}) collective-permute-start(f32[2,256]{1,0:T(2,128)S(1)} %reduce_sum.9.near), channel_id=1, source_target_pairs={{0,2},{1,3},{2,0},{3,1},{4,6},{5,7},{6,4},{7,5},{8,10},{9,11},{10,... | collective-permute-start | bytes 6152 | tf_op jit(solution)/shard_map/ppermute | solution.py:328
  28.9 0.0 copy-done
  28.9 0.0 copy-done.1
  28.9 0.0 copy-done.2
  28.9 0.0 copy-done.6
  28.9 0.3 shard_map.163
  29.3 0.0 copy-done.3
  29.3 0.0 copy-done.4
  29.3 0.3 shard_map.164.mix_cols
  29.6 1.2 %collective-permute-done.far = f32[2,256]{1,0:T(2,128)S(1)} collective-permute-done((f32[2,256]{1,0:T(2,128)S(1)}, f32[2,256]{1,0:T(2,128)S(1)}, u32[]{:S(2)}, u32[]{:S(2)}) %collective-permute-start) | collective-permute-done | bytes 2080 | tf_op jit(solution)/shard_map/ppermute | solution.py:328
  30.8 0.9 shard_map.165
  31.7 0.0 copy-start.5
  31.7 11.1 %all-to-all-start.1 = ((bf16[32,64,128]{2,1,0:T(8,128)(2,1)}), bf16[32,64,128]{2,1,0:T(8,128)(2,1)S(1)}, u32[]{:S(2)}, u32[]{:S(2)}) async-start(bf16[32,64,128]{2,1,0:T(8,128)(2,1)} %shard_map.165), calls=%async_computation.1 | async-start | bytes 1048576 | tf_op jit(solution)/shard_map/all_to_all | solution.py:384
  42.8 0.0 copy-done.5
  42.8 0.6 shard_map.166.filt
  43.4 1.1 %shard_map.162 = (bf16[256,512]{1,0:T(8,128)(2,1)}, f32[1,512]{1,0:T(1,128)S(1)}) custom-call(bf16[256,512]{1,0:T(8,128)(2,1)S(1)} %copy-done, bf16[256,512]{1,0:T(8,128)(2,1)S(1)} %copy-done.1, bf16[256,512]{1,0:T(8,128)(2,1)S(1)} %copy-done.2, f32[1,512]{1,0:T(1,128)S(1)} %copy-done.6, f32[2,256]{1,0:T(2,128)S(1)} %reduce_sum.9.near, ...), custom_call_target="tpu_custom_call" | custom-call | bytes 1056768 | tf_op jit(solution)/shard_map/pallas_call | solution.py:37
  44.5 0.0 copy-start.8
  44.5 0.0 copy-start.9
  44.5 27.4 %all-to-all-done.1.cols = bf16[32,64,128]{2,1,0:T(8,128)(2,1)S(1)} async-done(((bf16[32,64,128]{2,1,0:T(8,128)(2,1)}), bf16[32,64,128]{2,1,0:T(8,128)(2,1)S(1)}, u32[]{:S(2)}, u32[]{:S(2)}) %all-to-all-start.1) | async-done | bytes 524320 | tf_op jit(solution)/shard_map/all_to_all | solution.py:384
  72.0 0.0 copy-done.8
  72.0 0.0 copy-done.9
  72.0 6.7 %shard_map.167 = (bf16[32,18,2,128]{3,2,1,0:T(2,128)(2,1)S(1)}, f32[16,8192]{1,0:T(8,128)}, f32[1,16]{1,0:T(1,128)}, f32[1,16]{1,0:T(1,128)}) custom-call(bf16[32,64,128]{2,1,0:T(8,128)(2,1)S(1)} %all-to-all-done.1.cols, bf16[32,32,128]{2,1,0:T(8,128)(2,1)S(1)} %shard_map.166.filt, f32[1,16]{1,0:T(1,128)S(1)} %copy-done.8, ...), custom_call_target="tpu_custom_call" | custom-call | flops 2147483648 | bytes 1607936 | tf_op jit(solution)/shard_map/pallas_call | solution.py:37
  78.7 0.0 copy-start.7
  78.7 25.6 %all_to_all.16.back = bf16[32,18,2,128]{3,2,1,0:T(2,128)(2,1)S(1)} all-to-all(bf16[32,18,2,128]{3,2,1,0:T(2,128)(2,1)S(1)} %get-tuple-element.24), channel_id=1, replica_groups=mesh['seq'=32,'ch'=16] {'seq'}, dimensions={0} | all-to-all | bytes 589824 | tf_op jit(solution)/shard_map/all_to_all | solution.py:388
  104.3 0.0 copy-done.7
  104.3 1.1 %shard_map.168 = (bf16[256,512]{1,0:T(8,128)(2,1)}, bf16[256,512]{1,0:T(8,128)(2,1)}, f32[1,256]{1,0:T(1,128)}, f32[1,16]{1,0:T(1,128)}) custom-call(bf16[32,18,2,128]{3,2,1,0:T(2,128)(2,1)S(1)} %all_to_all.16.back, bf16[256,512]{1,0:T(8,128)(2,1)S(1)} %copy-done.3, bf16[256,512]{1,0:T(8,128)(2,1)S(1)} %copy-done.4, f32[1,256]{1,0:T(1,128)S(1)} %copy-done.7), custom_call_target="tpu_custom_call" | custom-call | bytes 1345600 | tf_op jit(solution)/shard_map/pallas_call | solution.py:37
  (1 shorter events, 0.0 us)
Async XLA Ops:
  0.6 28.2 %copy-start = (bf16[256,512]{1,0:T(8,128)(2,1)S(1)}, bf16[256,512]{1,0:T(8,128)(2,1)}, u32[]{:S(2)}) copy-start(bf16[256,512]{1,0:T(8,128)(2,1)} %query.3) | copy-start | bytes 786436
  0.6 28.2 %copy-start.1 = (bf16[256,512]{1,0:T(8,128)(2,1)S(1)}, bf16[256,512]{1,0:T(8,128)(2,1)}, u32[]{:S(2)}) copy-start(bf16[256,512]{1,0:T(8,128)(2,1)} %conv.3) | copy-start | bytes 786436
  0.7 28.2 %copy-start.2 = (bf16[256,512]{1,0:T(8,128)(2,1)S(1)}, bf16[256,512]{1,0:T(8,128)(2,1)}, u32[]{:S(2)}) copy-start(bf16[256,512]{1,0:T(8,128)(2,1)} %cot.3) | copy-start | bytes 786436
  17.6 11.3 %copy-start.6 = (f32[1,512]{1,0:T(1,128)S(1)}, f32[1,512]{1,0:T(1,128)}, u32[]{:S(2)}) copy-start(f32[1,512]{1,0:T(1,128)} %gain.3) | copy-start | bytes 6148
  17.6 11.7 %copy-start.3 = (bf16[256,512]{1,0:T(8,128)(2,1)S(1)}, bf16[256,512]{1,0:T(8,128)(2,1)}, u32[]{:S(2)}) copy-start(bf16[256,512]{1,0:T(8,128)(2,1)} %key.3) | copy-start | bytes 786436
  17.6 11.7 %copy-start.4 = (bf16[256,512]{1,0:T(8,128)(2,1)S(1)}, bf16[256,512]{1,0:T(8,128)(2,1)}, u32[]{:S(2)}) copy-start(bf16[256,512]{1,0:T(8,128)(2,1)} %value.3) | copy-start | bytes 786436
  17.6 13.2 %collective-permute-start = (f32[2,256]{1,0:T(2,128)S(1)}, f32[2,256]{1,0:T(2,128)S(1)}, u32[]{:S(2)}, u32[]{:S(2)}) collective-permute-start(f32[2,256]{1,0:T(2,128)S(1)} %reduce_sum.9.near), channel_id=1, source_target_pairs={{0,2},{1,3},{2,0},{3,1},{4,6},{5,7},{6,4},{7,5},{8,10},{9,11},{10,... | collective-permute-start | bytes 6152 | tf_op jit(solution)/shard_map/ppermute | solution.py:328
  31.7 11.1 %copy-start.5 = (f32[1,16,8192]{2,1,0:T(8,128)S(1)}, f32[1,16,8192]{2,1,0:T(8,128)}, u32[]{:S(2)}) copy-start(f32[1,16,8192]{2,1,0:T(8,128)} %param.17) | copy-start | bytes 1572868
  31.7 40.3 %all-to-all-start.1 = ((bf16[32,64,128]{2,1,0:T(8,128)(2,1)}), bf16[32,64,128]{2,1,0:T(8,128)(2,1)S(1)}, u32[]{:S(2)}, u32[]{:S(2)}) async-start(bf16[32,64,128]{2,1,0:T(8,128)(2,1)} %shard_map.165), calls=%async_computation.1 | async-start | bytes 1048576 | tf_op jit(solution)/shard_map/all_to_all | solution.py:384
  44.5 27.4 %copy-start.8 = (f32[1,16]{1,0:T(1,128)S(1)}, f32[1,16]{1,0:T(1,128)}, u32[]{:S(2)}) copy-start(f32[1,16]{1,0:T(1,128)} %skip.1) | copy-start | bytes 196
  44.5 27.4 %copy-start.9 = (f32[1,16]{1,0:T(1,128)S(1)}, f32[1,16]{1,0:T(1,128)}, u32[]{:S(2)}) copy-start(f32[1,16]{1,0:T(1,128)} %col_prev.1) | copy-start | bytes 196
  78.7 25.6 %copy-start.7 = (f32[1,256]{1,0:T(1,128)S(1)}, f32[1,256]{1,0:T(1,128)}, u32[]{:S(2)}) copy-start(f32[1,256]{1,0:T(1,128)} %row_prev.1) | copy-start | bytes 3076

commit v7 on v6

--- a/solution.py
+++ b/solution.py
@@ -32,13 +32,15 @@
     return jnp.where(token == source, 1.0, 0.0).astype(BF16)
 
 
-def kernel_call(body, outs, args, scratch=(), flops=0, in_place=(), vmem=16 << 20):
+def kernel_call(body, outs, args, scratch=(), flops=0, in_place=(), out_place=(), vmem=16 << 20):
     total = sum(math.prod(a.shape) * a.dtype.itemsize for a in list(args) + list(outs))
     return pl.pallas_call(
         body,
         out_shape=tuple(outs),
         in_specs=[pl.BlockSpec(memory_space=pl.ANY if i in in_place else pltpu.VMEM) for i in range(len(args))],
-        out_specs=tuple(pl.BlockSpec(memory_space=pltpu.VMEM) for _ in outs),
+        out_specs=tuple(
+            pl.BlockSpec(memory_space=pl.ANY if i in out_place else pltpu.VMEM) for i in range(len(outs))
+        ),
         scratch_shapes=list(scratch),
         compiler_params=pltpu.CompilerParams(vmem_limit_bytes=vmem),
         cost_estimate=pl.CostEstimate(flops=flops, bytes_accessed=total, transcendentals=0),
@@ -115,15 +117,25 @@
     return inv, inv * inv * (totals[1:2, :] / total_width)
 
 
-def send_columns(total_width, plain, gated_q, near, far, mix_cols, cols):
+def send_columns(total_width, plain, gated_q, near, far, mix_cols, cols_at, cols, sems):
+    peers, chunk = cols.shape[0], 16
+    copies = [pltpu.make_async_copy(mix_cols, cols_at.at[:, pl.ds(32, 32), :], sems.at[peers // chunk])]
+    copies[0].start()
     inv, back = token_scales(total_width, near, far)
-    cols[:, 32:64, :] = mix_cols[...]
-    for half in range(plain.shape[1] // LANE):
-        lo = slice(half * LANE, (half + 1) * LANE)
-        for d in range(cols.shape[0]):
-            at = (slice(d * 16, d * 16 + 16), lo)
-            grad = inv[:, lo] * (plain[at] - back[:, lo] * gated_q[at])
-            cols[d, half * 16 : half * 16 + 16, :] = grad.astype(BF16)
+    for first in range(0, peers, chunk):
+        for half in range(plain.shape[1] // LANE):
+            lo = slice(half * LANE, (half + 1) * LANE)
+            for d in range(first, first + chunk):
+                at = (slice(d * 16, d * 16 + 16), lo)
+                grad = inv[:, lo] * (plain[at] - back[:, lo] * gated_q[at])
+                cols[d, half * 16 : half * 16 + 16, :] = grad.astype(BF16)
+        mine = pl.ds(first, chunk)
+        copies.append(
+            pltpu.make_async_copy(cols.at[mine], cols_at.at[mine, pl.ds(0, 32), :], sems.at[first // chunk])
+        )
+        copies[-1].start()
+    for copy in copies:
+        copy.wait()
 
 
 def token_grads(total_width, query, conv, cot, gain, near, far, grad_query, gain_part):
@@ -375,6 +387,8 @@
         functools.partial(send_columns, group * n_ch),
         [shape((n_seq, 64, LANE), BF16)],
         [plain, gated_q, near, far, mix_cols],
+        [pltpu.VMEM((n_seq, 32, LANE), BF16), pltpu.SemaphoreType.DMA((n_seq // 16 + 1,))],
+        out_place=(0,),
     )
     grad_query, gain_part = kernel_call(
         functools.partial(token_grads, group * n_ch),

time: 106 us -> 106 us (level)
  no operation moved by 1% of the time
where the time goes in v7:
time: 106 us; the launch traced here: 105 us
  blocking collectives  40.4 us (38%)
  waiting for transfers between devices  28.6 us (27%)
  starting transfers between devices  22.4 us (21%)
  Pallas kernels  13.1 us (12%)
    all_to_all x1, waiting for transfers between devices, body(): cols = lax.all_to_all(cols, 'seq', split_axis=0, concat_axis=0, tiled=True)  27.4 us
    all_to_all x1, blocking collectives, body(): back = lax.all_to_all(back, 'seq', split_axis=0, concat_axis=0, tiled=True)  25.6 us
    all_to_all x1, blocking collectives, sum_over_channels(): lax.all_to_all(sums, 'ch', split_axis=0, concat_axis=0, axis_index_groups...  14.8 us
    pallas_call x8, Pallas kernels, kernel_call(): pl.pallas_call(body, out_shape=tuple(outs), in_specs=[pl.BlockSpec(memory...  13.1 us
    ppermute x1, starting transfers between devices, sum_over_channels(): return (here, lax.ppermute(here, 'ch', [(i, i ^ 2) for i in range(16)]))  11.3 us
    all_to_all x1, starting transfers between devices, body(): cols = lax.all_to_all(cols, 'seq', split_axis=0, concat_axis=0, tiled=True)  11.1 us
  transfers between devices with their start and end apart: 2, of which 2 were waited for; matrix products, arithmetic and copies ran while one was open for 0% of the time, Pallas kernels for 2%

profile of v7, /device:TPU:1, one launch (start us, length us, event | category | flops | bytes accessed | tf_op | source)
XLA Modules:
  0.0 105.3 jit_solution(2970291480886106356)
XLA Ops:
  0.6 0.0 copy-start
  0.6 0.0 copy-start.1
  0.7 0.0 copy-start.2
  0.7 2.1 %shard_map.161 = f32[8,2,256]{2,1,0:T(2,128)} custom-call(bf16[256,512]{1,0:T(8,128)(2,1)} %query.3, bf16[256,512]{1,0:T(8,128)(2,1)} %conv.3, bf16[256,512]{1,0:T(8,128)(2,1)} %cot.3, f32[1,512]{1,0:T(1,128)} %gain.3), custom_call_target="tpu_custom_call" | custom-call | bytes 804864 | tf_op jit(solution)/shard_map/pallas_call | solution.py:37
  2.8 14.8 %all_to_all.15 = f32[8,2,256]{2,1,0:T(2,128)S(1)} all-to-all(f32[8,2,256]{2,1,0:T(2,128)} %shard_map.161), channel_id=1, replica_groups={{0,1,4,5,8,9,12,13},{2,3,6,7,10,11,14,15},{16,17,20,21,24,25,28,29},{18..., dimensions={0} | all-to-all | bytes 32768 | tf_op jit(solution)/shard_map/all_to_all | solution.py:338
  17.6 0.0 copy-start.6
  17.6 0.0 copy-start.3
  17.6 0.0 copy-start.4
  17.6 11.3 %collective-permute-start = (f32[2,256]{1,0:T(2,128)S(1)}, f32[2,256]{1,0:T(2,128)S(1)}, u32[]{:S(2)}, u32[]{:S(2)}) collective-permute-start(f32[2,256]{1,0:T(2,128)S(1)} %reduce_sum.9.near), channel_id=1, source_target_pairs={{0,2},{1,3},{2,0},{3,1},{4,6},{5,7},{6,4},{7,5},{8,10},{9,11},{10,... | collective-permute-start | bytes 6152 | tf_op jit(solution)/shard_map/ppermute | solution.py:340
  28.9 0.0 copy-done
  28.9 0.0 copy-done.1
  28.9 0.0 copy-done.2
  28.9 0.0 copy-done.6
  28.9 0.3 shard_map.163
  29.3 0.0 copy-done.3
  29.3 0.0 copy-done.4
  29.3 0.3 shard_map.164.mix_cols
  29.6 1.2 %collective-permute-done.far = f32[2,256]{1,0:T(2,128)S(1)} collective-permute-done((f32[2,256]{1,0:T(2,128)S(1)}, f32[2,256]{1,0:T(2,128)S(1)}, u32[]{:S(2)}, u32[]{:S(2)}) %collective-permute-start) | collective-permute-done | bytes 2080 | tf_op jit(solution)/shard_map/ppermute | solution.py:340
  30.8 0.8 shard_map.165
  31.6 0.0 copy-start.5
  31.6 11.1 %all-to-all-start.1 = ((bf16[32,64,128]{2,1,0:T(8,128)(2,1)}), bf16[32,64,128]{2,1,0:T(8,128)(2,1)S(1)}, u32[]{:S(2)}, u32[]{:S(2)}) async-start(bf16[32,64,128]{2,1,0:T(8,128)(2,1)} %shard_map.165), calls=%async_computation.1 | async-start | bytes 1048576 | tf_op jit(solution)/shard_map/all_to_all | solution.py:398
  42.7 0.0 copy-done.5
  42.7 0.6 shard_map.166.filt
  43.4 1.1 %shard_map.162 = (bf16[256,512]{1,0:T(8,128)(2,1)}, f32[1,512]{1,0:T(1,128)S(1)}) custom-call(bf16[256,512]{1,0:T(8,128)(2,1)S(1)} %copy-done, bf16[256,512]{1,0:T(8,128)(2,1)S(1)} %copy-done.1, bf16[256,512]{1,0:T(8,128)(2,1)S(1)} %copy-done.2, f32[1,512]{1,0:T(1,128)S(1)} %copy-done.6, f32[2,256]{1,0:T(2,128)S(1)} %reduce_sum.9.near, ...), custom_call_target="tpu_custom_call" | custom-call | bytes 1056768 | tf_op jit(solution)/shard_map/pallas_call | solution.py:37
  44.5 0.0 copy-start.8
  44.5 0.0 copy-start.9
  44.5 27.4 %all-to-all-done.1.cols = bf16[32,64,128]{2,1,0:T(8,128)(2,1)S(1)} async-done(((bf16[32,64,128]{2,1,0:T(8,128)(2,1)}), bf16[32,64,128]{2,1,0:T(8,128)(2,1)S(1)}, u32[]{:S(2)}, u32[]{:S(2)}) %all-to-all-start.1) | async-done | bytes 524320 | tf_op jit(solution)/shard_map/all_to_all | solution.py:398
  71.9 0.0 copy-done.8
  71.9 0.0 copy-done.9
  71.9 6.7 %shard_map.167 = (bf16[32,18,2,128]{3,2,1,0:T(2,128)(2,1)S(1)}, f32[16,8192]{1,0:T(8,128)}, f32[1,16]{1,0:T(1,128)}, f32[1,16]{1,0:T(1,128)}) custom-call(bf16[32,64,128]{2,1,0:T(8,128)(2,1)S(1)} %all-to-all-done.1.cols, bf16[32,32,128]{2,1,0:T(8,128)(2,1)S(1)} %shard_map.166.filt, f32[1,16]{1,0:T(1,128)S(1)} %copy-done.8, ...), custom_call_target="tpu_custom_call" | custom-call | flops 2147483648 | bytes 1607936 | tf_op jit(solution)/shard_map/pallas_call | solution.py:37
  78.6 0.0 copy-start.7
  78.6 25.6 %all_to_all.16.back = bf16[32,18,2,128]{3,2,1,0:T(2,128)(2,1)S(1)} all-to-all(bf16[32,18,2,128]{3,2,1,0:T(2,128)(2,1)S(1)} %get-tuple-element.24), channel_id=1, replica_groups=mesh['seq'=32,'ch'=16] {'seq'}, dimensions={0} | all-to-all | bytes 589824 | tf_op jit(solution)/shard_map/all_to_all | solution.py:402
  104.3 0.0 copy-done.7
  104.3 1.1 %shard_map.168 = (bf16[256,512]{1,0:T(8,128)(2,1)}, bf16[256,512]{1,0:T(8,128)(2,1)}, f32[1,256]{1,0:T(1,128)}, f32[1,16]{1,0:T(1,128)}) custom-call(bf16[32,18,2,128]{3,2,1,0:T(2,128)(2,1)S(1)} %all_to_all.16.back, bf16[256,512]{1,0:T(8,128)(2,1)S(1)} %copy-done.3, bf16[256,512]{1,0:T(8,128)(2,1)S(1)} %copy-done.4, f32[1,256]{1,0:T(1,128)S(1)} %copy-done.7), custom_call_target="tpu_custom_call" | custom-call | bytes 1345600 | tf_op jit(solution)/shard_map/pallas_call | solution.py:37
  (1 shorter events, 0.0 us)
Async XLA Ops:
  0.6 28.2 %copy-start = (bf16[256,512]{1,0:T(8,128)(2,1)S(1)}, bf16[256,512]{1,0:T(8,128)(2,1)}, u32[]{:S(2)}) copy-start(bf16[256,512]{1,0:T(8,128)(2,1)} %query.3) | copy-start | bytes 786436
  0.6 28.2 %copy-start.1 = (bf16[256,512]{1,0:T(8,128)(2,1)S(1)}, bf16[256,512]{1,0:T(8,128)(2,1)}, u32[]{:S(2)}) copy-start(bf16[256,512]{1,0:T(8,128)(2,1)} %conv.3) | copy-start | bytes 786436
  0.7 28.2 %copy-start.2 = (bf16[256,512]{1,0:T(8,128)(2,1)S(1)}, bf16[256,512]{1,0:T(8,128)(2,1)}, u32[]{:S(2)}) copy-start(bf16[256,512]{1,0:T(8,128)(2,1)} %cot.3) | copy-start | bytes 786436
  17.6 11.3 %copy-start.6 = (f32[1,512]{1,0:T(1,128)S(1)}, f32[1,512]{1,0:T(1,128)}, u32[]{:S(2)}) copy-start(f32[1,512]{1,0:T(1,128)} %gain.3) | copy-start | bytes 6148
  17.6 11.7 %copy-start.3 = (bf16[256,512]{1,0:T(8,128)(2,1)S(1)}, bf16[256,512]{1,0:T(8,128)(2,1)}, u32[]{:S(2)}) copy-start(bf16[256,512]{1,0:T(8,128)(2,1)} %key.3) | copy-start | bytes 786436
  17.6 11.7 %copy-start.4 = (bf16[256,512]{1,0:T(8,128)(2,1)S(1)}, bf16[256,512]{1,0:T(8,128)(2,1)}, u32[]{:S(2)}) copy-start(bf16[256,512]{1,0:T(8,128)(2,1)} %value.3) | copy-start | bytes 786436
  17.6 13.2 %collective-permute-start = (f32[2,256]{1,0:T(2,128)S(1)}, f32[2,256]{1,0:T(2,128)S(1)}, u32[]{:S(2)}, u32[]{:S(2)}) collective-permute-start(f32[2,256]{1,0:T(2,128)S(1)} %reduce_sum.9.near), channel_id=1, source_target_pairs={{0,2},{1,3},{2,0},{3,1},{4,6},{5,7},{6,4},{7,5},{8,10},{9,11},{10,... | collective-permute-start | bytes 6152 | tf_op jit(solution)/shard_map/ppermute | solution.py:340
  31.6 11.1 %copy-start.5 = (f32[1,16,8192]{2,1,0:T(8,128)S(1)}, f32[1,16,8192]{2,1,0:T(8,128)}, u32[]{:S(2)}) copy-start(f32[1,16,8192]{2,1,0:T(8,128)} %param.17) | copy-start | bytes 1572868
  31.6 40.3 %all-to-all-start.1 = ((bf16[32,64,128]{2,1,0:T(8,128)(2,1)}), bf16[32,64,128]{2,1,0:T(8,128)(2,1)S(1)}, u32[]{:S(2)}, u32[]{:S(2)}) async-start(bf16[32,64,128]{2,1,0:T(8,128)(2,1)} %shard_map.165), calls=%async_computation.1 | async-start | bytes 1048576 | tf_op jit(solution)/shard_map/all_to_all | solution.py:398
  44.5 27.4 %copy-start.8 = (f32[1,16]{1,0:T(1,128)S(1)}, f32[1,16]{1,0:T(1,128)}, u32[]{:S(2)}) copy-start(f32[1,16]{1,0:T(1,128)} %skip.1) | copy-start | bytes 196
  44.5 27.4 %copy-start.9 = (f32[1,16]{1,0:T(1,128)S(1)}, f32[1,16]{1,0:T(1,128)}, u32[]{:S(2)}) copy-start(f32[1,16]{1,0:T(1,128)} %col_prev.1) | copy-start | bytes 196
  78.6 25.6 %copy-start.7 = (f32[1,256]{1,0:T(1,128)S(1)}, f32[1,256]{1,0:T(1,128)}, u32[]{:S(2)}) copy-start(f32[1,256]{1,0:T(1,128)} %row_prev.1) | copy-start | bytes 3076
